TPU v7x, 32 devices: a whole 2x2x4 slice. The times are simulated.
32 devices in a mesh: feat: 16 (over z, y, x), frame: 2 (over core).
Axes of the slice: x: 2, y: 2, z: 4, core: 2. Of those that a mesh axis runs over, the one named last changes fastest.
Arguments:
- frames: float32 [6144, 440], P(('frame', 'feat')), may hold values from -6 to 6
- labels: int32 [6144], P('frame'), may hold values from 0 to 146, as said below
- proj: float32 [440, 32768], P(None, 'feat'), may hold values from -1 to 1
- phase: float32 [32768], P('feat'), may hold values from 0 to 6.2832
- class_weights: float32 [32768, 147], P('feat'), may hold values from -40 to 40
- velocity: float32 [32768, 147], P('feat'), may hold values from -3 to 3
Outputs:
- weights_out: float32 [32768, 147], P('feat')
- velocity_out: float32 [32768, 147], P('feat')
Inputs may be any that keep to these rules, and one draw needn't show every extreme that they name: labels come in runs of 4 to 12 consecutive frames that share one class (phone segments); neighbouring runs may share a class.
All inputs are finite; a program needn't handle non-finite values.
Results may differ from a plain program's by a relative error of at most 0.00011.
Values sent between devices are 32-bit elements; how exact they have to be, the bound alone decides.
No kernel may reach another device: no remote copies, remote signals or barrier semaphores. Data moves between devices by JAX's collectives and lax.ppermute only.
A program may use at most 128 MiB of HBM per device.

v0:
```python
import functools
import math

import jax
import jax.numpy as jnp
from jax import lax
from jax.experimental import pallas as pl
from jax.experimental.pallas import tpu as pltpu
from jax.sharding import PartitionSpec as P

ITERS = 2


MOMENTUM = 0.9
STEP_RATE = 0.05
EPSILON = 1e-06

BF16 = jnp.bfloat16
F32 = jnp.float32
NN = (((1,), (0,)), ((), ()))
NT = (((1,), (1,)), ((), ()))
MAGIC = 12582912.0
TURN = 1.0 / (2.0 * math.pi)
COS = (
    0.9999992107823203,
    -19.73898035576386,
    64.92865742102978,
    -85.2716215342655,
    58.790492119989025,
    -21.071105627426505,
)
VMEM_FEATURES = 12 * 2**20
VMEM_PRODUCTS = 8 * 2**20
VMEM_RESIDUAL = 4 * 2**20
VMEM_STEP = 8 * 2**20


def split(value):
    high = value.astype(BF16)
    return high, (value - high.astype(F32)).astype(BF16)


def split_array(value):
    high = lax.reduce_precision(value, exponent_bits=8, mantissa_bits=7)
    return high.astype(BF16), (value - high).astype(BF16)


def dot(left, right, dims):
    return lax.dot_general(left, right, dims, preferred_element_type=F32)


def cos_turns(turns):
    rest = turns - ((turns + MAGIC) - MAGIC)
    square = rest * rest
    total = jnp.float32(COS[-1])
    for factor in COS[-2::-1]:
        total = total * square + jnp.float32(factor)
    return total


def pad_rows(count):
    return -(-count // 8) * 8


def tree_edges(bits):
    loads, free, arrival, edges = [0] * bits, [0] * bits, {0: 0}, []
    for level in range(1, bits + 1):
        nodes = [n for n in range(1 << bits) if n.bit_count() == level]
        for node in sorted(nodes, key=lambda n: -n):
            choices = [b for b in range(bits) if node >> b & 1]
            if len(choices) > 1 and choices[-1] == bits - 1:
                choices = choices[:-1]
            bit = min(choices, key=lambda b: loads[b])
            loads[bit] += 1
            edges.append((bit, node ^ (1 << bit), node))
    ordered = []
    while edges:
        ready = [e for e in edges if e[1] in arrival]
        cost = lambda e: max(arrival[e[1]], free[e[0]]) + 1 + (e[0] == bits - 1)
        edge = min(ready, key=lambda e: (cost(e), -sum(e[2] & c[2] == e[2] for c in edges)))
        arrival[edge[2]] = free[edge[0]] = cost(edge)
        edges.remove(edge)
        ordered.append(edge)
    return ordered, arrival


def swap(value, axis, bit):
    count = lax.axis_size(axis)
    return lax.ppermute(value, axis, [(i, i ^ (1 << bit)) for i in range(count)])


def spread(item, axis, bits):
    known = {0: item}
    for bit, parent, child in tree_edges(len(bits))[0]:
        known[child] = swap(known[parent], axis, bits[bit])
    return known


def gather_sum(items, axis, bits):
    total = dict(items)
    for bit, parent, child in reversed(tree_edges(len(bits))[0]):
        total[parent] = total[parent] + swap(total[child], axis, bits[bit])
    return total[0]


def units_of(axis):
    bits = lax.axis_size(axis).bit_length() - 1
    arrival = tree_edges(bits)[1]
    blocks = [(u, u | 1 << bits - 1) for u in range(1 << bits - 1)]
    order = sorted(range(1, len(blocks)), key=lambda u: (max(arrival[j] for j in blocks[u]), -u))
    groups = [[(u, None) for u in order[i : i + 2]] for i in range(0, len(order), 2)]
    groups[0].append((0, 1))
    return blocks, [[(0, 0)]] + groups


def blocks_in(blocks, group):
    return [j for unit, half in group for j in (blocks[unit] if half is None else blocks[unit][half : half + 1])]


def widths_of(group, columns):
    return [2 * columns if half is None else columns for _, half in group]


def hand_out(total, refs):
    left = 0
    for ref in refs:
        ref[...] = total[:, left : left + ref.shape[1]]
        left += ref.shape[1]


def features_kernel(*refs, arrays, after, width):
    frames, refs = refs[:arrays], refs[arrays:]
    p_high, p_low, phase, look, look_high = refs[:5]
    high, low, *scores, x_parts, total = refs[5 + after :]
    rows = look_high.shape[0]
    top = 0
    for array in frames:
        part = slice(top, top + array.shape[0])
        x_parts[0, part], x_parts[1, part] = split(array[...])
        top = part.stop

    total[...] = jnp.zeros(total.shape, F32)

    def chunk(i, carry):
        part = pl.ds(pl.multiple_of(i * width, width), width)
        turns = (
            dot(x_parts[0], p_high[:, part], NN)
            + dot(x_parts[0], p_low[:, part], NN)
            + dot(x_parts[1], p_high[:, part], NN)
        )
        f_high, f_low = split(cos_turns(turns + phase[:, part]))
        high[:, part] = f_high
        low[:, part] = f_low
        both = dot(look[:, part], f_high, NT)
        total[...] += both[:rows] + both[rows:] + dot(look_high[:, part], f_low, NT)
        return carry

    lax.fori_loop(0, high.shape[1] // width, chunk, 0)
    hand_out(total, scores)


def features_call(frames, proj, phase, look, after, widths, width):
    count, depth = sum(widths), frames[0].shape[1]
    feats = proj[0].shape[1]
    rows = look[1].shape[0]
    whole = pl.BlockSpec(memory_space=pltpu.VMEM)
    return pl.pallas_call(
        functools.partial(features_kernel, arrays=len(frames), after=len(after), width=width),
        in_specs=[whole] * (len(frames) + 5) + [pl.BlockSpec(memory_space=pl.ANY)] * len(after),
        out_specs=[whole] * (2 + len(widths)),
        out_shape=[jax.ShapeDtypeStruct((count, feats), BF16)] * 2
        + [jax.ShapeDtypeStruct((rows, columns), F32) for columns in widths],
        scratch_shapes=[pltpu.VMEM((2, count, depth), BF16), pltpu.VMEM((rows, count), F32)],
        compiler_params=pltpu.CompilerParams(vmem_limit_bytes=VMEM_FEATURES),
        cost_estimate=pl.CostEstimate(
            flops=6 * count * feats * (depth + rows), bytes_accessed=4 * count * feats, transcendentals=0
        ),
        name="features",
    )(*frames, *proj, phase, *look, *after)


def scores_kernel(look, look_high, high, low, _, *scores):
    rows = look_high.shape[0]
    both = dot(look[...], high[...], NT)
    hand_out(both[:rows] + both[rows:] + dot(look_high[...], low[...], NT), scores)


def scores_call(look, high, low, after, widths):
    count, feats = high.shape
    rows = look[1].shape[0]
    whole = pl.BlockSpec(memory_space=pltpu.VMEM)
    return pl.pallas_call(
        scores_kernel,
        in_specs=[whole] * 4 + [pl.BlockSpec(memory_space=pl.ANY)],
        out_specs=[whole] * len(widths),
        out_shape=[jax.ShapeDtypeStruct((rows, columns), F32) for columns in widths],
        compiler_params=pltpu.CompilerParams(vmem_limit_bytes=VMEM_PRODUCTS),
        cost_estimate=pl.CostEstimate(
            flops=6 * count * feats * rows, bytes_accessed=4 * count * feats, transcendentals=0
        ),
        name="scores",
    )(*look, high, low, after)


def gradient_kernel(*refs, halves, first, step):
    units = len(halves)
    residual, refs = refs[:units], refs[units:]
    if first:
        high, low, gradient, parts = refs
    else:
        high, low, before, gradient, parts = refs
    rows = gradient.shape[0]
    left = 0
    for ref, half in zip(residual, halves):
        value = ref[...]
        if half is not None:
            columns = value.shape[1] // 2
            value = value[:, half * columns : (half + 1) * columns]
        parts[:, left : left + value.shape[1]] = jnp.concatenate(split(value), axis=0)
        left += value.shape[1]

    def chunk(i, _):
        part = pl.ds(pl.multiple_of(i * step, step), step)
        both = dot(parts[...], high[:, part], NN)
        value = both[:rows] + both[rows:] + dot(parts[:rows], low[:, part], NN)
        gradient[:, part] = value if first else before[:, part] + value
        return _

    lax.fori_loop(0, gradient.shape[1] // step, chunk, 0)


def gradient_call(residual, halves, high, low, before, step):
    units = len(residual)
    rows = residual[0].shape[0]
    count, feats = high.shape
    first = before is None
    whole = pl.BlockSpec(memory_space=pltpu.VMEM)
    return pl.pallas_call(
        functools.partial(gradient_kernel, halves=halves, first=first, step=step),
        in_specs=[whole] * (units + 2 + (not first)),
        out_specs=whole,
        out_shape=jax.ShapeDtypeStruct((rows, feats), F32),
        input_output_aliases={} if first else {units + 2: 0},
        scratch_shapes=[pltpu.VMEM((2 * rows, count), BF16)],
        compiler_params=pltpu.CompilerParams(vmem_limit_bytes=VMEM_PRODUCTS),
        cost_estimate=pl.CostEstimate(
            flops=6 * count * feats * rows, bytes_accessed=4 * count * feats, transcendentals=0
        ),
        name="gradient",
    )(*residual, high, low, *([] if first else [before]))


def residual_kernel(mine, theirs, labels, residual, *, classes, scale):
    half = mine.shape[1] // 2
    row = lax.broadcasted_iota(jnp.int32, mine.shape, 0)
    turned = jnp.concatenate([theirs[:, half:], theirs[:, :half]], axis=1)
    value = jnp.where(row < classes, (mine[...] + turned) * F32(scale), -jnp.inf)
    exponent = jnp.exp(value - jnp.max(value, axis=0, keepdims=True))
    probability = exponent / jnp.sum(exponent, axis=0, keepdims=True)
    residual[...] = probability - (row == labels[...]).astype(F32)


def residual_call(mine, theirs, labels, classes, scale):
    return pl.pallas_call(
        functools.partial(residual_kernel, classes=classes, scale=scale),
        out_shape=jax.ShapeDtypeStruct(mine.shape, F32),
        compiler_params=pltpu.CompilerParams(vmem_limit_bytes=VMEM_RESIDUAL),
        name="residual",
    )(mine, theirs, labels)


def total_kernel(mine, theirs, gradient, tiles, *, scale):
    value = (mine[...] + theirs[...]) * F32(scale)
    gradient[...] = value
    tiles[...] = jnp.broadcast_to(jnp.sum(value * value), tiles.shape)


def total_call(mine, theirs, devices, scale):
    whole = pl.BlockSpec(memory_space=pltpu.VMEM)
    return pl.pallas_call(
        functools.partial(total_kernel, scale=scale),
        in_specs=[whole] * 2,
        out_specs=[whole] * 2,
        out_shape=[jax.ShapeDtypeStruct(mine.shape, F32), jax.ShapeDtypeStruct((devices, 8, 128), F32)],
        compiler_params=pltpu.CompilerParams(vmem_limit_bytes=VMEM_STEP),
        name="total",
    )(mine, theirs)


def look_kernel(weights, velocity, look, look_high):
    write_look(weights[...] + F32(MOMENTUM) * velocity[...], look, look_high)


def write_look(value, look, look_high):
    classes, feats = value.shape
    rows = look_high.shape[0]
    if rows > classes:
        value = jnp.concatenate([value, jnp.zeros((rows - classes, feats), F32)], axis=0)
    high, low = split(value)
    look[...] = jnp.concatenate([high, low], axis=0)
    look_high[...] = high


def step_kernel(tiles, gradient, weights, velocity, weights_out, velocity_out, *looks, count):
    classes = weights.shape[0]
    squares = jnp.sum(tiles[...], axis=0)[:1, :1]
    rate = F32(STEP_RATE) / jnp.sqrt(squares / F32(count) + F32(EPSILON))
    velocity_now = F32(MOMENTUM) * velocity[...] - gradient[:classes] * rate
    weights_now = weights[...] + velocity_now
    velocity_out[...] = velocity_now
    weights_out[...] = weights_now
    if looks:
        write_look(weights_now + F32(MOMENTUM) * velocity_now, *looks)


def looks_of(weights):
    rows, feats = pad_rows(weights.shape[0]), weights.shape[1]
    return [jax.ShapeDtypeStruct((2 * rows, feats), BF16), jax.ShapeDtypeStruct((rows, feats), BF16)]


def look_call(weights, velocity):
    whole = pl.BlockSpec(memory_space=pltpu.VMEM)
    return pl.pallas_call(
        look_kernel,
        in_specs=[whole] * 2,
        out_specs=[whole] * 2,
        out_shape=looks_of(weights),
        compiler_params=pltpu.CompilerParams(vmem_limit_bytes=VMEM_STEP),
        name="look",
    )(weights, velocity)


def step_call(tiles, gradient, weights, velocity, count, last):
    whole = pl.BlockSpec(memory_space=pltpu.VMEM)
    out_shape = [jax.ShapeDtypeStruct(weights.shape, F32)] * 2 + ([] if last else looks_of(weights))
    return pl.pallas_call(
        functools.partial(step_kernel, count=count),
        in_specs=[whole] * 4,
        out_specs=[whole] * len(out_shape),
        out_shape=out_shape,
        compiler_params=pltpu.CompilerParams(vmem_limit_bytes=VMEM_STEP),
        name="step",
    )(tiles, gradient, weights, velocity)


def first_scores(known, proj_parts, phase_turns, look, ready, blocks, groups):
    count = lax.axis_size("feat")
    columns = known[0].shape[0]
    parts, own, others, arrived, after = [], [], [], [], [ready]
    for group in groups:
        here = [known[j] for j in blocks_in(blocks, group)]
        high, low, *sums = features_call(
            here, proj_parts, phase_turns, look, after, widths_of(group, columns), 512
        )
        parts.append((high, low))
        after = [sums[0]] + arrived
        arrived = []
        for (unit, _), value in zip(group, sums):
            if unit == 0:
                own.append(value)
            else:
                arrived.append(lax.ppermute(value, "feat", [(i, i ^ unit) for i in range(count)]))
        others += arrived
    return parts, sum(others, jnp.concatenate(own, axis=1))


def next_scores(parts, look, groups, columns):
    after, own, found = look[1], [], {}
    for group, (high, low) in zip(reversed(groups), reversed(parts)):
        sums = scores_call(look, high, low, after, widths_of(group, columns))
        after = sums[0]
        for (unit, half), value in zip(group, sums):
            found[unit, half] = value
    found[0, None] = jnp.concatenate([found.pop((0, 0)), found.pop((0, 1))], axis=1)
    bits = lax.axis_size("feat").bit_length() - 2
    return gather_sum({unit: value for (unit, _), value in found.items()}, "feat", list(range(bits)))


def on_device(frames, labels, proj, phase, class_weights, velocity):
    feat_count = lax.axis_size("feat") * proj.shape[1]
    classes = class_weights.shape[1]
    feat_scale = math.sqrt(2.0 / feat_count)
    count_all = feat_count * classes
    columns = frames.shape[0]
    bits = lax.axis_size("feat").bit_length() - 1
    blocks, groups = units_of("feat")
    me = lax.axis_index("feat")
    labels_own = jnp.concatenate(
        [lax.dynamic_slice(labels, (owner * columns,), (columns,)) for owner in (me, me ^ (1 << bits - 1))]
    )[None, :]
    known = spread(frames, "feat", list(range(bits)))
    proj_parts = split_array(proj * F32(TURN))
    phase_turns = (phase * F32(TURN))[None, :]
    weights_now = class_weights.T
    velocity_now = velocity.T
    look = look_call(weights_now, velocity_now)
    for iteration in range(ITERS):
        if iteration == 0:
            parts, mine = first_scores(known, proj_parts, phase_turns, look, labels_own, blocks, groups)
        else:
            mine = next_scores(parts, look, groups, columns)
        residual = residual_call(mine, swap(mine, "feat", bits - 1), labels_own, classes, feat_scale)
        residual = spread(residual, "feat", list(range(bits - 1)))
        gradient = None
        for group, (high, low) in zip(groups, parts):
            gradient = gradient_call(
                [residual[u] for u, _ in group], [half for _, half in group], high, low, gradient, 1024
            )
        gradient, tiles = total_call(gradient, swap(gradient, "frame", 0), 1 << bits, feat_scale)
        tiles = lax.all_to_all(tiles, "feat", 0, 0)
        weights_now, velocity_now, *look = step_call(
            tiles, gradient, weights_now, velocity_now, count_all, iteration == ITERS - 1
        )
    return (weights_now.T, velocity_now.T)


def solution(mesh):
    return jax.shard_map(
        on_device,
        mesh=mesh,
        in_specs=(
            P(("frame", "feat"), None),
            P("frame"),
            P(None, "feat"),
            P("feat"),
            P("feat", None),
            P("feat", None),
        ),
        out_specs=(P("feat", None), P("feat", None)),
        check_vma=False,
    )
```

profile of v0, /device:TPU:0, one launch (start us, length us, event | category | flops | bytes accessed | tf_op | source)
XLA Modules:
  0.0 219.1 jit_solution(14882000767433950479)
XLA Ops:
  0.6 4.1 %collective-permute-start.1 = (f32[192,440]{1,0:T(8,128)}, f32[192,440]{1,0:T(8,128)S(1)}, u32[]{:S(2)}, u32[]{:S(2)}) collective-permute-start(f32[192,440]{1,0:T(8,128)} %refs_0_.1), channel_id=1, source_target_pairs={{0,16},{2,18},{4,20},{6,22},{8,24},{10,26},{12,28},{14,30},{16,0},... | collective-permute-start | bytes 1013768 | tf_op jit(solution)/shard_map/ppermute | solution.py:89
  13.2 2.8 %fusion = (bf16[440,2048]{1,0:T(8,128)(2,1)S(1)}, bf16[440,2048]{1,0:T(8,128)(2,1)S(1)}) fusion(f32[440,2048]{1,0:T(8,128)} %param.8), kind=kLoop, calls=%fused_computation.2 | loop fusion | flops 4505600 | bytes 7208960 | tf_op jit(solution)/shard_map/convert_element_type | solution.py:45
  16.1 6.5 %collective-permute-done.1.refs_4_ = f32[192,440]{1,0:T(8,128)S(1)} collective-permute-done((f32[192,440]{1,0:T(8,128)}, f32[192,440]{1,0:T(8,128)S(1)}, u32[]{:S(2)}, u32[]{:S(2)}) %collective-permute-start.1) | collective-permute-done | bytes 337952 | tf_op jit(solution)/shard_map/ppermute | solution.py:89
  24.8 3.7 %features.5 = (bf16[192,2048]{1,0:T(8,128)(2,1)S(1)}, bf16[192,2048]{1,0:T(8,128)(2,1)S(1)}, f32[152,192]{1,0:T(8,128)S(1)}) custom-call(f32[192,440]{1,0:T(8,128)S(1)} %copy-done.4, bf16[440,2048]{1,0:T(8,128)(2,1)S(1)} %get-tuple-element.79.refs_1_.refs_5_.refs_4_.refs_2_, bf16[440,2048]{1,0:T(8,128)(2,1)S(1)} %get-tuple-element.78.refs_2_.refs_6_.refs_5_.refs_3_, ...), custom_call_target="tpu_custom_call" | custom-call | flops 1396703232 | bytes 1572864 | tf_op jit(solution)/shard_map/features/pallas_call | solution.py:167
  30.7 2.2 collective-permute-done.4.refs_3_
  35.9 13.1 %features.6 = (bf16[960,2048]{1,0:T(8,128)(2,1)S(1)}, bf16[960,2048]{1,0:T(8,128)(2,1)S(1)}, f32[152,384]{1,0:T(8,128)S(1)}, f32[152,384]{1,0:T(8,128)S(1)}, f32[152,192]{1,0:T(8,128)S(1)}) custom-call(f32[192,440]{1,0:T(8,128)S(1)} %collective-permute-done.refs_0_, f32[192,440]{1,0:T(8,128)S(1)} %collective-permute-done.2.refs_1_, ...), custom_call_target="tpu_custom_call" | custom-call | flops 6983516160 | bytes 7864320 | tf_op jit(solution)/shard_map/features/pallas_call | solution.py:167
  54.6 10.6 %features.7 = (bf16[768,2048]{1,0:T(8,128)(2,1)S(1)}, bf16[768,2048]{1,0:T(8,128)(2,1)S(1)}, f32[152,384]{1,0:T(8,128)S(1)}, f32[152,384]{1,0:T(8,128)S(1)}) custom-call(f32[192,440]{1,0:T(8,128)S(1)} %collective-permute-done.7.refs_0_, f32[192,440]{1,0:T(8,128)S(1)} %collective-permute-done.8.refs_1_, f32[192,440]{1,0:T(8,128)S(1)} %collective-permute-done.9.refs_2_, ...), custom_call_target="tpu_custom_call" | custom-call | flops 5586812928 | bytes 6291456 | tf_op jit(solution)/shard_map/features/pallas_call | solution.py:167
  69.0 10.6 %features.8 = (bf16[768,2048]{1,0:T(8,128)(2,1)S(1)}, bf16[768,2048]{1,0:T(8,128)(2,1)S(1)}, f32[152,384]{1,0:T(8,128)S(1)}, f32[152,384]{1,0:T(8,128)S(1)}) custom-call(f32[192,440]{1,0:T(8,128)S(1)} %collective-permute-done.13.refs_0_, f32[192,440]{1,0:T(8,128)S(1)} %collective-permute-done.14.refs_1_, f32[192,440]{1,0:T(8,128)S(1)} %collective-permute-done.15.refs_2_, ...), custom_call_target="tpu_custom_call" | custom-call | flops 5586812928 | bytes 6291456 | tf_op jit(solution)/shard_map/features/pallas_call | solution.py:167
  82.9 6.2 %features.9 = (bf16[384,2048]{1,0:T(8,128)(2,1)S(1)}, bf16[384,2048]{1,0:T(8,128)(2,1)S(1)}, f32[152,384]{1,0:T(8,128)S(1)}) custom-call(f32[192,440]{1,0:T(8,128)S(1)} %collective-permute-done.19.refs_0_, f32[192,440]{1,0:T(8,128)S(1)} %collective-permute-done.20.refs_1_, bf16[440,2048]{1,0:T(8,128)(2,1)S(1)} %get-tuple-element.79.refs_1_.refs_5_.refs_4_.refs_2_, ...), custom_call_target="tpu_custom_call" | custom-call | flops 2793406464 | bytes 3145728 | tf_op jit(solution)/shard_map/features/pallas_call | solution.py:167
  91.9 5.1 %collective-permute-done.21 = f32[152,384]{1,0:T(8,128)S(1)} collective-permute-done((f32[152,384]{1,0:T(8,128)S(1)}, f32[152,384]{1,0:T(8,128)S(1)}, u32[]{:S(2)}, u32[]{:S(2)}) %collective-permute-start.21) | collective-permute-done | bytes 233504 | tf_op jit(solution)/shard_map/ppermute | solution.py:362
  97.2 5.2 %collective-permute-start.22 = (f32[152,384]{1,0:T(8,128)S(1)}, f32[152,384]{1,0:T(8,128)S(1)}, u32[]{:S(2)}, u32[]{:S(2)}) collective-permute-start(f32[152,384]{1,0:T(8,128)S(1)} %fusion.6.mine), channel_id=1, source_target_pairs={{0,16},{2,18},{4,20},{6,22},{8,24},{10,26},{12,28},{14,30},{16,0},... | collective-permute-start | bytes 700424 | tf_op jit(solution)/shard_map/ppermute | solution.py:89
  102.4 5.4 %collective-permute-done.22.theirs = f32[152,384]{1,0:T(8,128)S(1)} collective-permute-done((f32[152,384]{1,0:T(8,128)S(1)}, f32[152,384]{1,0:T(8,128)S(1)}, u32[]{:S(2)}, u32[]{:S(2)}) %collective-permute-start.22) | collective-permute-done | bytes 233504 | tf_op jit(solution)/shard_map/ppermute | solution.py:89
  108.8 5.4 %collective-permute-done.23.refs_0_ = f32[152,384]{1,0:T(8,128)S(1)} collective-permute-done((f32[152,384]{1,0:T(8,128)S(1)}, f32[152,384]{1,0:T(8,128)S(1)}, u32[]{:S(2)}, u32[]{:S(2)}) %collective-permute-start.23) | collective-permute-done | bytes 233504 | tf_op jit(solution)/shard_map/ppermute | solution.py:89
  119.1 2.7 %gradient.11.refs_4_ = f32[152,2048]{1,0:T(8,128)S(1)} custom-call(f32[152,384]{1,0:T(8,128)S(1)} %collective-permute-done.23.refs_0_, f32[152,384]{1,0:T(8,128)S(1)} %collective-permute-done.26.refs_1_, f32[152,384]{1,0:T(8,128)S(1)} %residual.2.refs_0_.refs_2_, ...), custom_call_target="tpu_custom_call", output_to_operand_aliasing={{}: (5, {})} | custom-call | flops 1793064960 | bytes 7864320 | tf_op jit(solution)/shard_map/gradient/pallas_call | solution.py:238
  123.3 2.0 gradient.12.refs_4_
  125.8 2.1 gradient.13.refs_3_
  129.5 2.9 %collective-permute-done.30.theirs = f32[152,2048]{1,0:T(8,128)S(1)} collective-permute-done((f32[152,2048]{1,0:T(8,128)S(1)}, f32[152,2048]{1,0:T(8,128)S(1)}, u32[]{:S(2)}, u32[]{:S(2)}) %collective-permute-start.30) | collective-permute-done | bytes 1245216 | tf_op jit(solution)/shard_map/ppermute | solution.py:89
  133.1 12.5 %all_to_all.10.tiles = f32[16,8,128]{2,1,0:T(8,128)S(1)} all-to-all(f32[16,8,128]{2,1,0:T(8,128)S(1)} %get-tuple-element.61), channel_id=1, replica_groups=mesh['feat'=16,'frame'=2] {'feat'}, dimensions={0} | all-to-all | bytes 131072 | tf_op jit(solution)/shard_map/all_to_all | solution.py:410
  148.5 2.0 scores.6
  151.2 2.0 scores.7
  157.1 2.7 %scores.8 = (f32[152,384]{1,0:T(8,128)S(1)}, f32[152,384]{1,0:T(8,128)S(1)}, f32[152,192]{1,0:T(8,128)S(1)}) custom-call(bf16[304,2048]{1,0:T(8,128)(2,1)S(1)} %get-tuple-element.63.look, bf16[152,2048]{1,0:T(8,128)(2,1)S(1)} %get-tuple-element.64.look_high._, bf16[960,2048]{1,0:T(8,128)(2,1)S(1)} %get-tuple-element.57.refs_3_.high, ...), custom_call_target="tpu_custom_call" | custom-call | flops 1793064960 | bytes 7864320 | tf_op jit(solution)/shard_map/scores/pallas_call | solution.py:192
  160.4 3.3 %collective-permute-done.32 = f32[152,384]{1,0:T(8,128)S(1)} collective-permute-done((f32[152,384]{1,0:T(8,128)S(1)}, f32[152,384]{1,0:T(8,128)S(1)}, u32[]{:S(2)}, u32[]{:S(2)}) %collective-permute-start.32) | collective-permute-done | bytes 233504 | tf_op jit(solution)/shard_map/ppermute | solution.py:89
  166.9 3.4 %collective-permute-done.34 = f32[152,384]{1,0:T(8,128)S(1)} collective-permute-done((f32[152,384]{1,0:T(8,128)S(1)}, f32[152,384]{1,0:T(8,128)S(1)}, u32[]{:S(2)}, u32[]{:S(2)}) %collective-permute-start.34) | collective-permute-done | bytes 233504 | tf_op jit(solution)/shard_map/ppermute | solution.py:89
  170.6 9.6 %collective-permute-done.38.theirs = f32[152,384]{1,0:T(8,128)S(1)} collective-permute-done((f32[152,384]{1,0:T(8,128)S(1)}, f32[152,384]{1,0:T(8,128)S(1)}, u32[]{:S(2)}, u32[]{:S(2)}) %collective-permute-start.38) | collective-permute-done | bytes 233504 | tf_op jit(solution)/shard_map/ppermute | solution.py:89
  180.4 3.1 %collective-permute-start.42 = (f32[152,384]{1,0:T(8,128)S(1)}, f32[152,384]{1,0:T(8,128)S(1)}, u32[]{:S(2)}, u32[]{:S(2)}) collective-permute-start(f32[152,384]{1,0:T(8,128)S(1)} %residual.3.refs_0_.refs_2_), channel_id=1, source_target_pairs={{0,4},{2,6},{4,0},{6,2},{8,12},{10,14},{12,8},{14,10},{16,20},{18,... | collective-permute-start | bytes 700424 | tf_op jit(solution)/shard_map/ppermute | solution.py:89
  183.6 2.9 %collective-permute-done.39.refs_0_ = f32[152,384]{1,0:T(8,128)S(1)} collective-permute-done((f32[152,384]{1,0:T(8,128)S(1)}, f32[152,384]{1,0:T(8,128)S(1)}, u32[]{:S(2)}, u32[]{:S(2)}) %collective-permute-start.39) | collective-permute-done | bytes 233504 | tf_op jit(solution)/shard_map/ppermute | solution.py:89
  186.5 2.4 %collective-permute-start.40 = (f32[152,384]{1,0:T(8,128)S(1)}, f32[152,384]{1,0:T(8,128)S(1)}, u32[]{:S(2)}, u32[]{:S(2)}) collective-permute-start(f32[152,384]{1,0:T(8,128)S(1)} %collective-permute-done.39.refs_0_), channel_id=1, source_target_pairs={{0,2},{2,0},{4,6},{6,4},{8,10},{10,8},{12,14},{14,12},{16,18},{18,... | collective-permute-start | bytes 700424 | tf_op jit(solution)/shard_map/ppermute | solution.py:89
  191.9 2.5 %gradient.16.refs_4_ = f32[152,2048]{1,0:T(8,128)S(1)} custom-call(f32[152,384]{1,0:T(8,128)S(1)} %collective-permute-done.39.refs_0_, f32[152,384]{1,0:T(8,128)S(1)} %collective-permute-done.42.refs_1_, f32[152,384]{1,0:T(8,128)S(1)} %residual.3.refs_0_.refs_2_, ...), custom_call_target="tpu_custom_call", output_to_operand_aliasing={{}: (5, {})} | custom-call | flops 1793064960 | bytes 7864320 | tf_op jit(solution)/shard_map/gradient/pallas_call | solution.py:238
  194.4 2.1 collective-permute-start.41
  198.9 2.3 %gradient.18.refs_3_ = f32[152,2048]{1,0:T(8,128)S(1)} custom-call(f32[152,384]{1,0:T(8,128)S(1)} %collective-permute-done.43.refs_0_, f32[152,384]{1,0:T(8,128)S(1)} %collective-permute-done.40.refs_1_, bf16[768,2048]{1,0:T(8,128)(2,1)S(1)} %get-tuple-element.53.refs_2_.high, ...), custom_call_target="tpu_custom_call", output_to_operand_aliasing={{}: (4, {})} | custom-call | flops 1434451968 | bytes 6291456 | tf_op jit(solution)/shard_map/gradient/pallas_call | solution.py:238
  202.7 2.9 %collective-permute-done.46.theirs = f32[152,2048]{1,0:T(8,128)S(1)} collective-permute-done((f32[152,2048]{1,0:T(8,128)S(1)}, f32[152,2048]{1,0:T(8,128)S(1)}, u32[]{:S(2)}, u32[]{:S(2)}) %collective-permute-start.46) | collective-permute-done | bytes 1245216 | tf_op jit(solution)/shard_map/ppermute | solution.py:89
  206.3 11.0 %all_to_all.11.tiles = f32[16,8,128]{2,1,0:T(8,128)S(1)} all-to-all(f32[16,8,128]{2,1,0:T(8,128)S(1)} %get-tuple-element.72), channel_id=1, replica_groups=mesh['feat'=16,'frame'=2] {'feat'}, dimensions={0} | all-to-all | bytes 131072 | tf_op jit(solution)/shard_map/all_to_all | solution.py:410
  (113 shorter events, 62.7 us)
Async XLA Ops:
  0.6 22.0 %collective-permute-start.1 = (f32[192,440]{1,0:T(8,128)}, f32[192,440]{1,0:T(8,128)S(1)}, u32[]{:S(2)}, u32[]{:S(2)}) collective-permute-start(f32[192,440]{1,0:T(8,128)} %refs_0_.1), channel_id=1, source_target_pairs={{0,16},{2,18},{4,20},{6,22},{8,24},{10,26},{12,28},{14,30},{16,0},... | collective-permute-start | bytes 1013768 | tf_op jit(solution)/shard_map/ppermute | solution.py:89
  4.7 23.8 %collective-permute-start = (f32[192,440]{1,0:T(8,128)}, f32[192,440]{1,0:T(8,128)S(1)}, u32[]{:S(2)}, u32[]{:S(2)}) collective-permute-start(f32[192,440]{1,0:T(8,128)} %refs_0_.1), channel_id=1, source_target_pairs={{0,8},{2,10},{4,12},{6,14},{8,0},{10,2},{12,4},{14,6},{16,24},{18,... | collective-permute-start | bytes 1013768 | tf_op jit(solution)/shard_map/ppermute | solution.py:89
  6.3 42.6 %collective-permute-start.7 = (f32[192,440]{1,0:T(8,128)}, f32[192,440]{1,0:T(8,128)S(1)}, u32[]{:S(2)}, u32[]{:S(2)}) collective-permute-start(f32[192,440]{1,0:T(8,128)} %refs_0_.1), channel_id=1, source_target_pairs={{0,2},{2,0},{4,6},{6,4},{8,10},{10,8},{12,14},{14,12},{16,18},{18,... | collective-permute-start | bytes 1013768 | tf_op jit(solution)/shard_map/ppermute | solution.py:89
  7.8 22.3 %collective-permute-start.3 = (f32[192,440]{1,0:T(8,128)}, f32[192,440]{1,0:T(8,128)S(1)}, u32[]{:S(2)}, u32[]{:S(2)}) collective-permute-start(f32[192,440]{1,0:T(8,128)} %refs_0_.1), channel_id=1, source_target_pairs={{0,4},{2,6},{4,0},{6,2},{8,12},{10,14},{12,8},{14,10},{16,20},{18,... | collective-permute-start | bytes 1013768 | tf_op jit(solution)/shard_map/ppermute | solution.py:89
  22.6 10.2 %collective-permute-start.4 = (f32[192,440]{1,0:T(8,128)S(1)}, f32[192,440]{1,0:T(8,128)S(1)}, u32[]{:S(2)}, u32[]{:S(2)}) collective-permute-start(f32[192,440]{1,0:T(8,128)S(1)} %collective-permute-done.1.refs_4_), channel_id=1, source_target_pairs={{0,4},{2,6},{4,0},{6,2},{8,12},{10,14},{12,8},{14,10},{16,20},{18,... | collective-permute-start | bytes 1013768 | tf_op jit(solution)/shard_map/ppermute | solution.py:89
  24.2 9.9 %collective-permute-start.2 = (f32[192,440]{1,0:T(8,128)S(1)}, f32[192,440]{1,0:T(8,128)S(1)}, u32[]{:S(2)}, u32[]{:S(2)}) collective-permute-start(f32[192,440]{1,0:T(8,128)S(1)} %collective-permute-done.1.refs_4_), channel_id=1, source_target_pairs={{0,8},{2,10},{4,12},{6,14},{8,0},{10,2},{12,4},{14,6},{16,24},{18,... | collective-permute-start | bytes 1013768 | tf_op jit(solution)/shard_map/ppermute | solution.py:89
  28.6 22.0 %collective-permute-start.8 = (f32[192,440]{1,0:T(8,128)S(1)}, f32[192,440]{1,0:T(8,128)S(1)}, u32[]{:S(2)}, u32[]{:S(2)}) collective-permute-start(f32[192,440]{1,0:T(8,128)S(1)} %collective-permute-done.1.refs_4_), channel_id=1, source_target_pairs={{0,2},{2,0},{4,6},{6,4},{8,10},{10,8},{12,14},{14,12},{16,18},{18,... | collective-permute-start | bytes 1013768 | tf_op jit(solution)/shard_map/ppermute | solution.py:89
  30.1 20.9 %collective-permute-start.15 = (f32[192,440]{1,0:T(8,128)S(1)}, f32[192,440]{1,0:T(8,128)S(1)}, u32[]{:S(2)}, u32[]{:S(2)}) collective-permute-start(f32[192,440]{1,0:T(8,128)S(1)} %collective-permute-done.refs_0_), channel_id=1, source_target_pairs={{0,2},{2,0},{4,6},{6,4},{8,10},{10,8},{12,14},{14,12},{16,18},{18,... | collective-permute-start | bytes 1013768 | tf_op jit(solution)/shard_map/ppermute | solution.py:89
  32.8 18.5 %collective-permute-start.9 = (f32[192,440]{1,0:T(8,128)S(1)}, f32[192,440]{1,0:T(8,128)S(1)}, u32[]{:S(2)}, u32[]{:S(2)}) collective-permute-start(f32[192,440]{1,0:T(8,128)S(1)} %collective-permute-done.refs_0_), channel_id=1, source_target_pairs={{0,4},{2,6},{4,0},{6,2},{8,12},{10,14},{12,8},{14,10},{16,20},{18,... | collective-permute-start | bytes 1013768 | tf_op jit(solution)/shard_map/ppermute | solution.py:89
  34.1 18.9 %collective-permute-start.10 = (f32[192,440]{1,0:T(8,128)S(1)}, f32[192,440]{1,0:T(8,128)S(1)}, u32[]{:S(2)}, u32[]{:S(2)}) collective-permute-start(f32[192,440]{1,0:T(8,128)S(1)} %collective-permute-done.4.refs_3_), channel_id=1, source_target_pairs={{0,8},{2,10},{4,12},{6,14},{8,0},{10,2},{12,4},{14,6},{16,24},{18,... | collective-permute-start | bytes 1013768 | tf_op jit(solution)/shard_map/ppermute | solution.py:89
  48.9 16.2 %collective-permute-start.13 = (f32[192,440]{1,0:T(8,128)S(1)}, f32[192,440]{1,0:T(8,128)S(1)}, u32[]{:S(2)}, u32[]{:S(2)}) collective-permute-start(f32[192,440]{1,0:T(8,128)S(1)} %collective-permute-done.3.refs_2_), channel_id=1, source_target_pairs={{0,2},{2,0},{4,6},{6,4},{8,10},{10,8},{12,14},{14,12},{16,18},{18,... | collective-permute-start | bytes 1013768 | tf_op jit(solution)/shard_map/ppermute | solution.py:89
  50.5 15.3 %collective-permute-start.6 = (f32[152,384]{1,0:T(8,128)S(1)}, f32[152,384]{1,0:T(8,128)S(1)}, u32[]{:S(2)}, u32[]{:S(2)}) collective-permute-start(f32[152,384]{1,0:T(8,128)S(1)} %get-tuple-element.45), channel_id=1, source_target_pairs={{0,4},{2,6},{4,0},{6,2},{8,12},{10,14},{12,8},{14,10},{16,20},{18,... | collective-permute-start | bytes 700424 | tf_op jit(solution)/shard_map/ppermute | solution.py:362
  51.0 15.2 %collective-permute-start.5 = (f32[152,384]{1,0:T(8,128)S(1)}, f32[152,384]{1,0:T(8,128)S(1)}, u32[]{:S(2)}, u32[]{:S(2)}) collective-permute-start(f32[152,384]{1,0:T(8,128)S(1)} %get-tuple-element.44.refs_9_), channel_id=1, source_target_pairs={{0,8},{2,10},{4,12},{6,14},{8,0},{10,2},{12,4},{14,6},{16,24},{18,... | collective-permute-start | bytes 700424 | tf_op jit(solution)/shard_map/ppermute | solution.py:362
  51.3 16.2 %collective-permute-start.16 = (f32[192,440]{1,0:T(8,128)S(1)}, f32[192,440]{1,0:T(8,128)S(1)}, u32[]{:S(2)}, u32[]{:S(2)}) collective-permute-start(f32[192,440]{1,0:T(8,128)S(1)} %collective-permute-done.8.refs_1_), channel_id=1, source_target_pairs={{0,8},{2,10},{4,12},{6,14},{8,0},{10,2},{12,4},{14,6},{16,24},{18,... | collective-permute-start | bytes 1013768 | tf_op jit(solution)/shard_map/ppermute | solution.py:89
  53.1 16.0 %collective-permute-start.14 = (f32[192,440]{1,0:T(8,128)S(1)}, f32[192,440]{1,0:T(8,128)S(1)}, u32[]{:S(2)}, u32[]{:S(2)}) collective-permute-start(f32[192,440]{1,0:T(8,128)S(1)} %collective-permute-done.8.refs_1_), channel_id=1, source_target_pairs={{0,4},{2,6},{4,0},{6,2},{8,12},{10,14},{12,8},{14,10},{16,20},{18,... | collective-permute-start | bytes 1013768 | tf_op jit(solution)/shard_map/ppermute | solution.py:89
  65.2 16.2 %collective-permute-start.19 = (f32[192,440]{1,0:T(8,128)S(1)}, f32[192,440]{1,0:T(8,128)S(1)}, u32[]{:S(2)}, u32[]{:S(2)}) collective-permute-start(f32[192,440]{1,0:T(8,128)S(1)} %collective-permute-done.9.refs_2_), channel_id=1, source_target_pairs={{0,2},{2,0},{4,6},{6,4},{8,10},{10,8},{12,14},{14,12},{16,18},{18,... | collective-permute-start | bytes 1013768 | tf_op jit(solution)/shard_map/ppermute | solution.py:89
  65.8 17.1 %collective-permute-start.12 = (f32[152,384]{1,0:T(8,128)S(1)}, f32[152,384]{1,0:T(8,128)S(1)}, u32[]{:S(2)}, u32[]{:S(2)}) collective-permute-start(f32[152,384]{1,0:T(8,128)S(1)} %get-tuple-element.47), channel_id=1, source_target_pairs={{0,12},{2,14},{4,8},{6,10},{8,4},{10,6},{12,0},{14,2},{16,28},{18,... | collective-permute-start | bytes 700424 | tf_op jit(solution)/shard_map/ppermute | solution.py:362
  66.2 16.6 %collective-permute-start.11 = (f32[152,384]{1,0:T(8,128)S(1)}, f32[152,384]{1,0:T(8,128)S(1)}, u32[]{:S(2)}, u32[]{:S(2)}) collective-permute-start(f32[152,384]{1,0:T(8,128)S(1)} %get-tuple-element.46.refs_9_), channel_id=1, source_target_pairs={{0,2},{2,0},{4,6},{6,4},{8,10},{10,8},{12,14},{14,12},{16,18},{18,... | collective-permute-start | bytes 700424 | tf_op jit(solution)/shard_map/ppermute | solution.py:362
  67.5 15.4 %collective-permute-start.20 = (f32[192,440]{1,0:T(8,128)S(1)}, f32[192,440]{1,0:T(8,128)S(1)}, u32[]{:S(2)}, u32[]{:S(2)}) collective-permute-start(f32[192,440]{1,0:T(8,128)S(1)} %collective-permute-done.16.refs_3_), channel_id=1, source_target_pairs={{0,4},{2,6},{4,0},{6,2},{8,12},{10,14},{12,8},{14,10},{16,20},{18,... | collective-permute-start | bytes 1013768 | tf_op jit(solution)/shard_map/ppermute | solution.py:89
  79.6 10.7 %collective-permute-start.18 = (f32[152,384]{1,0:T(8,128)S(1)}, f32[152,384]{1,0:T(8,128)S(1)}, u32[]{:S(2)}, u32[]{:S(2)}) collective-permute-start(f32[152,384]{1,0:T(8,128)S(1)} %get-tuple-element.49), channel_id=1, source_target_pairs={{0,10},{2,8},{4,14},{6,12},{8,2},{10,0},{12,6},{14,4},{16,26},{18,... | collective-permute-start | bytes 700424 | tf_op jit(solution)/shard_map/ppermute | solution.py:362
  81.4 10.5 %collective-permute-start.17 = (f32[152,384]{1,0:T(8,128)S(1)}, f32[152,384]{1,0:T(8,128)S(1)}, u32[]{:S(2)}, u32[]{:S(2)}) collective-permute-start(f32[152,384]{1,0:T(8,128)S(1)} %get-tuple-element.48.refs_7_), channel_id=1, source_target_pairs={{0,6},{2,4},{4,2},{6,0},{8,14},{10,12},{12,10},{14,8},{16,22},{18,... | collective-permute-start | bytes 700424 | tf_op jit(solution)/shard_map/ppermute | solution.py:362
  89.0 8.0 %collective-permute-start.21 = (f32[152,384]{1,0:T(8,128)S(1)}, f32[152,384]{1,0:T(8,128)S(1)}, u32[]{:S(2)}, u32[]{:S(2)}) collective-permute-start(f32[152,384]{1,0:T(8,128)S(1)} %get-tuple-element.50), channel_id=1, source_target_pairs={{0,14},{2,12},{4,10},{6,8},{8,6},{10,4},{12,2},{14,0},{16,30},{18,... | collective-permute-start | bytes 700424 | tf_op jit(solution)/shard_map/ppermute | solution.py:362
  97.2 10.7 %collective-permute-start.22 = (f32[152,384]{1,0:T(8,128)S(1)}, f32[152,384]{1,0:T(8,128)S(1)}, u32[]{:S(2)}, u32[]{:S(2)}) collective-permute-start(f32[152,384]{1,0:T(8,128)S(1)} %fusion.6.mine), channel_id=1, source_target_pairs={{0,16},{2,18},{4,20},{6,22},{8,24},{10,26},{12,28},{14,30},{16,0},... | collective-permute-start | bytes 700424 | tf_op jit(solution)/shard_map/ppermute | solution.py:89
  108.1 9.6 %collective-permute-start.26 = (f32[152,384]{1,0:T(8,128)S(1)}, f32[152,384]{1,0:T(8,128)S(1)}, u32[]{:S(2)}, u32[]{:S(2)}) collective-permute-start(f32[152,384]{1,0:T(8,128)S(1)} %residual.2.refs_0_.refs_2_), channel_id=1, source_target_pairs={{0,4},{2,6},{4,0},{6,2},{8,12},{10,14},{12,8},{14,10},{16,20},{18,... | collective-permute-start | bytes 700424 | tf_op jit(solution)/shard_map/ppermute | solution.py:89
  114.9 8.4 %collective-permute-start.28 = (f32[152,384]{1,0:T(8,128)S(1)}, f32[152,384]{1,0:T(8,128)S(1)}, u32[]{:S(2)}, u32[]{:S(2)}) collective-permute-start(f32[152,384]{1,0:T(8,128)S(1)} %residual.2.refs_0_.refs_2_), channel_id=1, source_target_pairs={{0,2},{2,0},{4,6},{6,4},{8,10},{10,8},{12,14},{14,12},{16,18},{18,... | collective-permute-start | bytes 700424 | tf_op jit(solution)/shard_map/ppermute | solution.py:89
  117.7 8.1 %collective-permute-start.27 = (f32[152,384]{1,0:T(8,128)S(1)}, f32[152,384]{1,0:T(8,128)S(1)}, u32[]{:S(2)}, u32[]{:S(2)}) collective-permute-start(f32[152,384]{1,0:T(8,128)S(1)} %collective-permute-done.26.refs_1_), channel_id=1, source_target_pairs={{0,2},{2,0},{4,6},{6,4},{8,10},{10,8},{12,14},{14,12},{16,18},{18,... | collective-permute-start | bytes 700424 | tf_op jit(solution)/shard_map/ppermute | solution.py:89
  150.6 9.2 %collective-permute-start.36 = (f32[152,384]{1,0:T(8,128)S(1)}, f32[152,384]{1,0:T(8,128)S(1)}, u32[]{:S(2)}, u32[]{:S(2)}) collective-permute-start(f32[152,384]{1,0:T(8,128)S(1)} %get-tuple-element.65._), channel_id=1, source_target_pairs={{0,2},{2,0},{4,6},{6,4},{8,10},{10,8},{12,14},{14,12},{16,18},{18,... | collective-permute-start | bytes 700424 | tf_op jit(solution)/shard_map/ppermute | solution.py:89
  155.0 8.7 %collective-permute-start.32 = (f32[152,384]{1,0:T(8,128)S(1)}, f32[152,384]{1,0:T(8,128)S(1)}, u32[]{:S(2)}, u32[]{:S(2)}) collective-permute-start(f32[152,384]{1,0:T(8,128)S(1)} %add.57), channel_id=1, source_target_pairs={{0,2},{2,0},{4,6},{6,4},{8,10},{10,8},{12,14},{14,12},{16,18},{18,... | collective-permute-start | bytes 700424 | tf_op jit(solution)/shard_map/ppermute | solution.py:89
  156.2 10.7 %collective-permute-start.35 = (f32[152,384]{1,0:T(8,128)S(1)}, f32[152,384]{1,0:T(8,128)S(1)}, u32[]{:S(2)}, u32[]{:S(2)}) collective-permute-start(f32[152,384]{1,0:T(8,128)S(1)} %get-tuple-element.66._), channel_id=1, source_target_pairs={{0,2},{2,0},{4,6},{6,4},{8,10},{10,8},{12,14},{14,12},{16,18},{18,... | collective-permute-start | bytes 700424 | tf_op jit(solution)/shard_map/ppermute | solution.py:89
  170.5 9.6 %collective-permute-start.38 = (f32[152,384]{1,0:T(8,128)S(1)}, f32[152,384]{1,0:T(8,128)S(1)}, u32[]{:S(2)}, u32[]{:S(2)}) collective-permute-start(f32[152,384]{1,0:T(8,128)S(1)} %fusion.8.mine), channel_id=1, source_target_pairs={{0,16},{2,18},{4,20},{6,22},{8,24},{10,26},{12,28},{14,30},{16,0},... | collective-permute-start | bytes 700424 | tf_op jit(solution)/shard_map/ppermute | solution.py:89
  180.4 10.5 %collective-permute-start.42 = (f32[152,384]{1,0:T(8,128)S(1)}, f32[152,384]{1,0:T(8,128)S(1)}, u32[]{:S(2)}, u32[]{:S(2)}) collective-permute-start(f32[152,384]{1,0:T(8,128)S(1)} %residual.3.refs_0_.refs_2_), channel_id=1, source_target_pairs={{0,4},{2,6},{4,0},{6,2},{8,12},{10,14},{12,8},{14,10},{16,20},{18,... | collective-permute-start | bytes 700424 | tf_op jit(solution)/shard_map/ppermute | solution.py:89
  190.9 8.0 %collective-permute-start.43 = (f32[152,384]{1,0:T(8,128)S(1)}, f32[152,384]{1,0:T(8,128)S(1)}, u32[]{:S(2)}, u32[]{:S(2)}) collective-permute-start(f32[152,384]{1,0:T(8,128)S(1)} %collective-permute-done.42.refs_1_), channel_id=1, source_target_pairs={{0,2},{2,0},{4,6},{6,4},{8,10},{10,8},{12,14},{14,12},{16,18},{18,... | collective-permute-start | bytes 700424 | tf_op jit(solution)/shard_map/ppermute | solution.py:89
  (21 other events, 155.2 us)
where the time goes:
time: 219 us
  Pallas kernels  75.7 us (35%)
  starting transfers between devices  57.1 us (26%)
  waiting for transfers between devices  55 us (25%)
  blocking collectives  23.5 us (11%)
  local copies, waits for them, and re-layouts  3.46 us (2%)
  other arithmetic  3.3 us (2%)
    ppermute x40, starting transfers between devices, swap(): return lax.ppermute(value, axis, [(i, i ^ 1 << bit) for i in range(count)])  50.1 us
    ppermute x40, waiting for transfers between devices, swap(): return lax.ppermute(value, axis, [(i, i ^ 1 << bit) for i in range(count)])  48.3 us
    pallas_call x5, Pallas kernels, features_call(): pl.pallas_call(functools.partial(features_kernel, arrays=len(frames), aft...  44.1 us
    all_to_all x2, blocking collectives, on_device(): tiles = lax.all_to_all(tiles, 'feat', 0, 0)  23.5 us
    pallas_call x10, Pallas kernels, gradient_call(): pl.pallas_call(functools.partial(gradient_kernel, halves=halves, first=fi...  18.1 us
    pallas_call x5, Pallas kernels, scores_call(): pl.pallas_call(scores_kernel, in_specs=[whole] * 4 + [pl.BlockSpec(memory...  8.72 us
    ppermute x7, starting transfers between devices, first_scores(): lax.ppermute(value, 'feat', [(i, i ^ unit) for i in range(count)])  6.96 us
    ppermute x7, waiting for transfers between devices, first_scores(): lax.ppermute(value, 'feat', [(i, i ^ unit) for i in range(count)])  6.69 us
  transfers between devices with their start and end apart: 47, of which 17 were waited for; matrix products, arithmetic and copies ran while one was open for 2% of the time, Pallas kernels for 31%

commit v1 on v0

--- a/solution.py
+++ b/solution.py
@@ -202,7 +202,7 @@
     )(*look, high, low, after)
 
 
-def gradient_kernel(*refs, halves, first, step):
+def gradient_kernel(*refs, halves, first, step, start):
     units = len(halves)
     residual, refs = refs[:units], refs[units:]
     if first:
@@ -220,27 +220,27 @@
         left += value.shape[1]
 
     def chunk(i, _):
-        part = pl.ds(pl.multiple_of(i * step, step), step)
+        part = pl.ds(pl.multiple_of(start + i * step, step), step)
         both = dot(parts[...], high[:, part], NN)
         value = both[:rows] + both[rows:] + dot(parts[:rows], low[:, part], NN)
-        gradient[:, part] = value if first else before[:, part] + value
+        gradient[:, pl.ds(pl.multiple_of(i * step, step), step)] = value if first else before[:, part] + value
         return _
 
     lax.fori_loop(0, gradient.shape[1] // step, chunk, 0)
 
 
-def gradient_call(residual, halves, high, low, before, step):
+def gradient_call(residual, halves, high, low, before, step, start=0, end=None):
     units = len(residual)
     rows = residual[0].shape[0]
     count, feats = high.shape
     first = before is None
     whole = pl.BlockSpec(memory_space=pltpu.VMEM)
     return pl.pallas_call(
-        functools.partial(gradient_kernel, halves=halves, first=first, step=step),
+        functools.partial(gradient_kernel, halves=halves, first=first, step=step, start=start),
         in_specs=[whole] * (units + 2 + (not first)),
         out_specs=whole,
-        out_shape=jax.ShapeDtypeStruct((rows, feats), F32),
-        input_output_aliases={} if first else {units + 2: 0},
+        out_shape=jax.ShapeDtypeStruct((rows, (end or feats) - start), F32),
+        input_output_aliases={} if first or end else {units + 2: 0},
         scratch_shapes=[pltpu.VMEM((2 * rows, count), BF16)],
         compiler_params=pltpu.CompilerParams(vmem_limit_bytes=VMEM_PRODUCTS),
         cost_estimate=pl.CostEstimate(
@@ -269,22 +269,31 @@
     )(mine, theirs, labels)
 
 
-def total_kernel(mine, theirs, gradient, tiles, *, scale):
-    value = (mine[...] + theirs[...]) * F32(scale)
-    gradient[...] = value
-    tiles[...] = jnp.broadcast_to(jnp.sum(value * value), tiles.shape)
-
-
-def total_call(mine, theirs, devices, scale):
-    whole = pl.BlockSpec(memory_space=pltpu.VMEM)
+def total_kernel(*refs, scale):
+    *halves, gradient, tiles = refs
+    left, squares = 0, 0.0
+    for mine, theirs in zip(halves[::2], halves[1::2]):
+        value = (mine[...] + theirs[...]) * F32(scale)
+        gradient[:, left : left + value.shape[1]] = value
+        left += value.shape[1]
+        squares += jnp.sum(value * value)
+    tiles[...] = jnp.broadcast_to(squares, tiles.shape)
+
+
+def total_call(halves, devices, scale):
+    whole = pl.BlockSpec(memory_space=pltpu.VMEM)
+    rows, feats = halves[0].shape[0], sum(half.shape[1] for half in halves[::2])
     return pl.pallas_call(
         functools.partial(total_kernel, scale=scale),
-        in_specs=[whole] * 2,
+        in_specs=[whole] * len(halves),
         out_specs=[whole] * 2,
-        out_shape=[jax.ShapeDtypeStruct(mine.shape, F32), jax.ShapeDtypeStruct((devices, 8, 128), F32)],
+        out_shape=[
+            jax.ShapeDtypeStruct((rows, feats), F32),
+            jax.ShapeDtypeStruct((devices, 8, 128), F32),
+        ],
         compiler_params=pltpu.CompilerParams(vmem_limit_bytes=VMEM_STEP),
         name="total",
-    )(mine, theirs)
+    )(*halves)
 
 
 def look_kernel(weights, velocity, look, look_high):
@@ -401,12 +410,17 @@
             mine = next_scores(parts, look, groups, columns)
         residual = residual_call(mine, swap(mine, "feat", bits - 1), labels_own, classes, feat_scale)
         residual = spread(residual, "feat", list(range(bits - 1)))
-        gradient = None
+        gradient, halves = None, []
         for group, (high, low) in zip(groups, parts):
-            gradient = gradient_call(
-                [residual[u] for u, _ in group], [half for _, half in group], high, low, gradient, 1024
-            )
-        gradient, tiles = total_call(gradient, swap(gradient, "frame", 0), 1 << bits, feat_scale)
+            here = [residual[u] for u, _ in group], [half for _, half in group], high, low
+            if group is groups[-1]:
+                middle = high.shape[1] // 2
+                for start in (0, middle):
+                    mine = gradient_call(*here, gradient, middle, start, start + middle)
+                    halves += [mine, swap(mine, "frame", 0)]
+            else:
+                gradient = gradient_call(*here, gradient, high.shape[1] // 2)
+        gradient, tiles = total_call(halves, 1 << bits, feat_scale)
         tiles = lax.all_to_all(tiles, "feat", 0, 0)
         weights_now, velocity_now, *look = step_call(
             tiles, gradient, weights_now, velocity_now, count_all, iteration == ITERS - 1

time: 219 us -> 217 us (level)
    ppermute x40 -> x42, waiting for transfers between devices: 48.3 us -> 46.8 us  [swap(): return lax.ppermute(value, axis, [(i, i ^ 1 << bit) for i in range(count)])]
    ppermute x40 -> x42, starting transfers between devices: 50.1 us -> 50.7 us  [swap(): return lax.ppermute(value, axis, [(i, i ^ 1 << bit) for i in range(count)])]
    pallas_call x10 -> x12, Pallas kernels: 18.1 us -> 17.9 us  [gradient_call(): pl.pallas_call(functools.partial(gradient_kernel, halves=halves, first=fi...]
  transfers between devices with their start and end apart: 47 -> 49, of which waited for: 17 -> 20; matrix products, arithmetic and copies ran while one was open for 2% -> 2% of each run, Pallas kernels for 31% -> 32%
where the time goes in v1:
time: 217 us
  Pallas kernels  75.1 us (35%)
  starting transfers between devices  57.6 us (27%)
  waiting for transfers between devices  53.4 us (25%)
  blocking collectives  23.1 us (11%)
  local copies, waits for them, and re-layouts  3.46 us (2%)
  other arithmetic  3.3 us (2%)
    ppermute x42, starting transfers between devices, swap(): return lax.ppermute(value, axis, [(i, i ^ 1 << bit) for i in range(count)])  50.7 us
    ppermute x42, waiting for transfers between devices, swap(): return lax.ppermute(value, axis, [(i, i ^ 1 << bit) for i in range(count)])  46.8 us
    pallas_call x5, Pallas kernels, features_call(): pl.pallas_call(functools.partial(features_kernel, arrays=len(frames), aft...  44.1 us
    all_to_all x2, blocking collectives, on_device(): tiles = lax.all_to_all(tiles, 'feat', 0, 0)  23.1 us
    pallas_call x12, Pallas kernels, gradient_call(): pl.pallas_call(functools.partial(gradient_kernel, halves=halves, first=fi...  17.9 us
    pallas_call x5, Pallas kernels, scores_call(): pl.pallas_call(scores_kernel, in_specs=[whole] * 4 + [pl.BlockSpec(memory...  8.7 us
    ppermute x7, starting transfers between devices, first_scores(): lax.ppermute(value, 'feat', [(i, i ^ unit) for i in range(count)])  6.97 us
    ppermute x7, waiting for transfers between devices, first_scores(): lax.ppermute(value, 'feat', [(i, i ^ unit) for i in range(count)])  6.67 us
  transfers between devices with their start and end apart: 49, of which 20 were waited for; matrix products, arithmetic and copies ran while one was open for 2% of the time, Pallas kernels for 32%

profile of v1, /device:TPU:0, one launch (start us, length us, event | category | flops | bytes accessed | tf_op | source)
XLA Modules:
  0.0 217.1 jit_solution(14480559360520599251)
XLA Ops:
  0.6 4.1 %collective-permute-start.1 = (f32[192,440]{1,0:T(8,128)}, f32[192,440]{1,0:T(8,128)S(1)}, u32[]{:S(2)}, u32[]{:S(2)}) collective-permute-start(f32[192,440]{1,0:T(8,128)} %refs_0_.1), channel_id=1, source_target_pairs={{0,16},{2,18},{4,20},{6,22},{8,24},{10,26},{12,28},{14,30},{16,0},... | collective-permute-start | bytes 1013768 | tf_op jit(solution)/shard_map/ppermute | solution.py:89
  13.2 2.8 %fusion = (bf16[440,2048]{1,0:T(8,128)(2,1)S(1)}, bf16[440,2048]{1,0:T(8,128)(2,1)S(1)}) fusion(f32[440,2048]{1,0:T(8,128)} %param.8), kind=kLoop, calls=%fused_computation.2 | loop fusion | flops 4505600 | bytes 7208960 | tf_op jit(solution)/shard_map/convert_element_type | solution.py:45
  16.1 6.5 %collective-permute-done.1.refs_4_ = f32[192,440]{1,0:T(8,128)S(1)} collective-permute-done((f32[192,440]{1,0:T(8,128)}, f32[192,440]{1,0:T(8,128)S(1)}, u32[]{:S(2)}, u32[]{:S(2)}) %collective-permute-start.1) | collective-permute-done | bytes 337952 | tf_op jit(solution)/shard_map/ppermute | solution.py:89
  24.8 3.7 %features.5 = (bf16[192,2048]{1,0:T(8,128)(2,1)S(1)}, bf16[192,2048]{1,0:T(8,128)(2,1)S(1)}, f32[152,192]{1,0:T(8,128)S(1)}) custom-call(f32[192,440]{1,0:T(8,128)S(1)} %copy-done.4, bf16[440,2048]{1,0:T(8,128)(2,1)S(1)} %get-tuple-element.79.refs_1_.refs_5_.refs_4_.refs_2_, bf16[440,2048]{1,0:T(8,128)(2,1)S(1)} %get-tuple-element.78.refs_2_.refs_6_.refs_5_.refs_3_, ...), custom_call_target="tpu_custom_call" | custom-call | flops 1396703232 | bytes 1572864 | tf_op jit(solution)/shard_map/features/pallas_call | solution.py:167
  30.7 2.2 %collective-permute-done.4.refs_3_ = f32[192,440]{1,0:T(8,128)S(1)} collective-permute-done((f32[192,440]{1,0:T(8,128)S(1)}, f32[192,440]{1,0:T(8,128)S(1)}, u32[]{:S(2)}, u32[]{:S(2)}) %collective-permute-start.4) | collective-permute-done | bytes 337952 | tf_op jit(solution)/shard_map/ppermute | solution.py:89
  34.1 1.8 collective-permute-start.10
  35.9 13.1 %features.6 = (bf16[960,2048]{1,0:T(8,128)(2,1)S(1)}, bf16[960,2048]{1,0:T(8,128)(2,1)S(1)}, f32[152,384]{1,0:T(8,128)S(1)}, f32[152,384]{1,0:T(8,128)S(1)}, f32[152,192]{1,0:T(8,128)S(1)}) custom-call(f32[192,440]{1,0:T(8,128)S(1)} %collective-permute-done.refs_0_, f32[192,440]{1,0:T(8,128)S(1)} %collective-permute-done.2.refs_1_, ...), custom_call_target="tpu_custom_call" | custom-call | flops 6983516160 | bytes 7864320 | tf_op jit(solution)/shard_map/features/pallas_call | solution.py:167
  54.6 10.6 %features.7 = (bf16[768,2048]{1,0:T(8,128)(2,1)S(1)}, bf16[768,2048]{1,0:T(8,128)(2,1)S(1)}, f32[152,384]{1,0:T(8,128)S(1)}, f32[152,384]{1,0:T(8,128)S(1)}) custom-call(f32[192,440]{1,0:T(8,128)S(1)} %collective-permute-done.7.refs_0_, f32[192,440]{1,0:T(8,128)S(1)} %collective-permute-done.8.refs_1_, f32[192,440]{1,0:T(8,128)S(1)} %collective-permute-done.9.refs_2_, ...), custom_call_target="tpu_custom_call" | custom-call | flops 5586812928 | bytes 6291456 | tf_op jit(solution)/shard_map/features/pallas_call | solution.py:167
  69.0 10.6 %features.8 = (bf16[768,2048]{1,0:T(8,128)(2,1)S(1)}, bf16[768,2048]{1,0:T(8,128)(2,1)S(1)}, f32[152,384]{1,0:T(8,128)S(1)}, f32[152,384]{1,0:T(8,128)S(1)}) custom-call(f32[192,440]{1,0:T(8,128)S(1)} %collective-permute-done.13.refs_0_, f32[192,440]{1,0:T(8,128)S(1)} %collective-permute-done.14.refs_1_, f32[192,440]{1,0:T(8,128)S(1)} %collective-permute-done.15.refs_2_, ...), custom_call_target="tpu_custom_call" | custom-call | flops 5586812928 | bytes 6291456 | tf_op jit(solution)/shard_map/features/pallas_call | solution.py:167
  79.6 1.8 collective-permute-start.18
  82.9 6.2 %features.9 = (bf16[384,2048]{1,0:T(8,128)(2,1)S(1)}, bf16[384,2048]{1,0:T(8,128)(2,1)S(1)}, f32[152,384]{1,0:T(8,128)S(1)}) custom-call(f32[192,440]{1,0:T(8,128)S(1)} %collective-permute-done.19.refs_0_, f32[192,440]{1,0:T(8,128)S(1)} %collective-permute-done.20.refs_1_, bf16[440,2048]{1,0:T(8,128)(2,1)S(1)} %get-tuple-element.79.refs_1_.refs_5_.refs_4_.refs_2_, ...), custom_call_target="tpu_custom_call" | custom-call | flops 2793406464 | bytes 3145728 | tf_op jit(solution)/shard_map/features/pallas_call | solution.py:167
  91.9 5.1 %collective-permute-done.21 = f32[152,384]{1,0:T(8,128)S(1)} collective-permute-done((f32[152,384]{1,0:T(8,128)S(1)}, f32[152,384]{1,0:T(8,128)S(1)}, u32[]{:S(2)}, u32[]{:S(2)}) %collective-permute-start.21) | collective-permute-done | bytes 233504 | tf_op jit(solution)/shard_map/ppermute | solution.py:371
  97.2 5.2 %collective-permute-start.22 = (f32[152,384]{1,0:T(8,128)S(1)}, f32[152,384]{1,0:T(8,128)S(1)}, u32[]{:S(2)}, u32[]{:S(2)}) collective-permute-start(f32[152,384]{1,0:T(8,128)S(1)} %fusion.6.mine), channel_id=1, source_target_pairs={{0,16},{2,18},{4,20},{6,22},{8,24},{10,26},{12,28},{14,30},{16,0},... | collective-permute-start | bytes 700424 | tf_op jit(solution)/shard_map/ppermute | solution.py:89
  102.4 5.4 %collective-permute-done.22.theirs = f32[152,384]{1,0:T(8,128)S(1)} collective-permute-done((f32[152,384]{1,0:T(8,128)S(1)}, f32[152,384]{1,0:T(8,128)S(1)}, u32[]{:S(2)}, u32[]{:S(2)}) %collective-permute-start.22) | collective-permute-done | bytes 233504 | tf_op jit(solution)/shard_map/ppermute | solution.py:89
  108.9 5.3 %collective-permute-done.23.refs_0_ = f32[152,384]{1,0:T(8,128)S(1)} collective-permute-done((f32[152,384]{1,0:T(8,128)S(1)}, f32[152,384]{1,0:T(8,128)S(1)}, u32[]{:S(2)}, u32[]{:S(2)}) %collective-permute-start.23) | collective-permute-done | bytes 233504 | tf_op jit(solution)/shard_map/ppermute | solution.py:89
  119.2 2.7 %gradient.13.refs_4_ = f32[152,2048]{1,0:T(8,128)S(1)} custom-call(f32[152,384]{1,0:T(8,128)S(1)} %collective-permute-done.23.refs_0_, f32[152,384]{1,0:T(8,128)S(1)} %collective-permute-done.26.refs_1_, f32[152,384]{1,0:T(8,128)S(1)} %residual.2.refs_0_.refs_2_, ...), custom_call_target="tpu_custom_call", output_to_operand_aliasing={{}: (5, {})} | custom-call | flops 1793064960 | bytes 7864320 | tf_op jit(solution)/shard_map/gradient/pallas_call | solution.py:238
  123.3 2.0 gradient.14.refs_4_
  125.8 2.0 gradient.15.refs_3_
  132.2 12.5 %all_to_all.10.tiles = f32[16,8,128]{2,1,0:T(8,128)S(1)} all-to-all(f32[16,8,128]{2,1,0:T(8,128)S(1)} %get-tuple-element.61), channel_id=1, replica_groups=mesh['feat'=16,'frame'=2] {'feat'}, dimensions={0} | all-to-all | bytes 131072 | tf_op jit(solution)/shard_map/all_to_all | solution.py:424
  147.6 2.0 scores.6
  150.3 2.0 scores.7
  156.2 2.7 %scores.8 = (f32[152,384]{1,0:T(8,128)S(1)}, f32[152,384]{1,0:T(8,128)S(1)}, f32[152,192]{1,0:T(8,128)S(1)}) custom-call(bf16[304,2048]{1,0:T(8,128)(2,1)S(1)} %get-tuple-element.63.look, bf16[152,2048]{1,0:T(8,128)(2,1)S(1)} %get-tuple-element.64.look_high._, bf16[960,2048]{1,0:T(8,128)(2,1)S(1)} %get-tuple-element.57.refs_3_.high, ...), custom_call_target="tpu_custom_call" | custom-call | flops 1793064960 | bytes 7864320 | tf_op jit(solution)/shard_map/scores/pallas_call | solution.py:192
  159.5 3.3 %collective-permute-done.33 = f32[152,384]{1,0:T(8,128)S(1)} collective-permute-done((f32[152,384]{1,0:T(8,128)S(1)}, f32[152,384]{1,0:T(8,128)S(1)}, u32[]{:S(2)}, u32[]{:S(2)}) %collective-permute-start.33) | collective-permute-done | bytes 233504 | tf_op jit(solution)/shard_map/ppermute | solution.py:89
  163.9 2.1 collective-permute-done.36
  166.0 3.7 %collective-permute-done.35 = f32[152,384]{1,0:T(8,128)S(1)} collective-permute-done((f32[152,384]{1,0:T(8,128)S(1)}, f32[152,384]{1,0:T(8,128)S(1)}, u32[]{:S(2)}, u32[]{:S(2)}) %collective-permute-start.35) | collective-permute-done | bytes 233504 | tf_op jit(solution)/shard_map/ppermute | solution.py:89
  169.9 9.0 %collective-permute-done.39.theirs = f32[152,384]{1,0:T(8,128)S(1)} collective-permute-done((f32[152,384]{1,0:T(8,128)S(1)}, f32[152,384]{1,0:T(8,128)S(1)}, u32[]{:S(2)}, u32[]{:S(2)}) %collective-permute-start.39) | collective-permute-done | bytes 233504 | tf_op jit(solution)/shard_map/ppermute | solution.py:89
  179.2 3.6 %collective-permute-start.43 = (f32[152,384]{1,0:T(8,128)S(1)}, f32[152,384]{1,0:T(8,128)S(1)}, u32[]{:S(2)}, u32[]{:S(2)}) collective-permute-start(f32[152,384]{1,0:T(8,128)S(1)} %residual.3.refs_0_.refs_2_), channel_id=1, source_target_pairs={{0,4},{2,6},{4,0},{6,2},{8,12},{10,14},{12,8},{14,10},{16,20},{18,... | collective-permute-start | bytes 700424 | tf_op jit(solution)/shard_map/ppermute | solution.py:89
  182.8 2.4 %collective-permute-done.40.refs_0_ = f32[152,384]{1,0:T(8,128)S(1)} collective-permute-done((f32[152,384]{1,0:T(8,128)S(1)}, f32[152,384]{1,0:T(8,128)S(1)}, u32[]{:S(2)}, u32[]{:S(2)}) %collective-permute-start.40) | collective-permute-done | bytes 233504 | tf_op jit(solution)/shard_map/ppermute | solution.py:89
  190.8 2.5 %gradient.19.refs_4_ = f32[152,2048]{1,0:T(8,128)S(1)} custom-call(f32[152,384]{1,0:T(8,128)S(1)} %collective-permute-done.40.refs_0_, f32[152,384]{1,0:T(8,128)S(1)} %collective-permute-done.43.refs_1_, f32[152,384]{1,0:T(8,128)S(1)} %residual.3.refs_0_.refs_2_, ...), custom_call_target="tpu_custom_call", output_to_operand_aliasing={{}: (5, {})} | custom-call | flops 1793064960 | bytes 7864320 | tf_op jit(solution)/shard_map/gradient/pallas_call | solution.py:238
  195.8 2.0 gradient.20.refs_4_
  198.3 2.2 %gradient.21.refs_3_ = f32[152,2048]{1,0:T(8,128)S(1)} custom-call(f32[152,384]{1,0:T(8,128)S(1)} %collective-permute-done.44.refs_0_, f32[152,384]{1,0:T(8,128)S(1)} %collective-permute-done.41.refs_1_, bf16[768,2048]{1,0:T(8,128)(2,1)S(1)} %get-tuple-element.53.refs_2_.high, ...), custom_call_target="tpu_custom_call", output_to_operand_aliasing={{}: (4, {})} | custom-call | flops 1434451968 | bytes 6291456 | tf_op jit(solution)/shard_map/gradient/pallas_call | solution.py:238
  204.7 10.7 %all_to_all.11.tiles = f32[16,8,128]{2,1,0:T(8,128)S(1)} all-to-all(f32[16,8,128]{2,1,0:T(8,128)S(1)} %get-tuple-element.72), channel_id=1, replica_groups=mesh['feat'=16,'frame'=2] {'feat'}, dimensions={0} | all-to-all | bytes 131072 | tf_op jit(solution)/shard_map/all_to_all | solution.py:424
  (119 shorter events, 64.3 us)
Async XLA Ops:
  0.6 22.0 %collective-permute-start.1 = (f32[192,440]{1,0:T(8,128)}, f32[192,440]{1,0:T(8,128)S(1)}, u32[]{:S(2)}, u32[]{:S(2)}) collective-permute-start(f32[192,440]{1,0:T(8,128)} %refs_0_.1), channel_id=1, source_target_pairs={{0,16},{2,18},{4,20},{6,22},{8,24},{10,26},{12,28},{14,30},{16,0},... | collective-permute-start | bytes 1013768 | tf_op jit(solution)/shard_map/ppermute | solution.py:89
  4.7 23.8 %collective-permute-start = (f32[192,440]{1,0:T(8,128)}, f32[192,440]{1,0:T(8,128)S(1)}, u32[]{:S(2)}, u32[]{:S(2)}) collective-permute-start(f32[192,440]{1,0:T(8,128)} %refs_0_.1), channel_id=1, source_target_pairs={{0,8},{2,10},{4,12},{6,14},{8,0},{10,2},{12,4},{14,6},{16,24},{18,... | collective-permute-start | bytes 1013768 | tf_op jit(solution)/shard_map/ppermute | solution.py:89
  6.3 42.6 %collective-permute-start.7 = (f32[192,440]{1,0:T(8,128)}, f32[192,440]{1,0:T(8,128)S(1)}, u32[]{:S(2)}, u32[]{:S(2)}) collective-permute-start(f32[192,440]{1,0:T(8,128)} %refs_0_.1), channel_id=1, source_target_pairs={{0,2},{2,0},{4,6},{6,4},{8,10},{10,8},{12,14},{14,12},{16,18},{18,... | collective-permute-start | bytes 1013768 | tf_op jit(solution)/shard_map/ppermute | solution.py:89
  7.8 22.3 %collective-permute-start.3 = (f32[192,440]{1,0:T(8,128)}, f32[192,440]{1,0:T(8,128)S(1)}, u32[]{:S(2)}, u32[]{:S(2)}) collective-permute-start(f32[192,440]{1,0:T(8,128)} %refs_0_.1), channel_id=1, source_target_pairs={{0,4},{2,6},{4,0},{6,2},{8,12},{10,14},{12,8},{14,10},{16,20},{18,... | collective-permute-start | bytes 1013768 | tf_op jit(solution)/shard_map/ppermute | solution.py:89
  22.6 10.2 %collective-permute-start.4 = (f32[192,440]{1,0:T(8,128)S(1)}, f32[192,440]{1,0:T(8,128)S(1)}, u32[]{:S(2)}, u32[]{:S(2)}) collective-permute-start(f32[192,440]{1,0:T(8,128)S(1)} %collective-permute-done.1.refs_4_), channel_id=1, source_target_pairs={{0,4},{2,6},{4,0},{6,2},{8,12},{10,14},{12,8},{14,10},{16,20},{18,... | collective-permute-start | bytes 1013768 | tf_op jit(solution)/shard_map/ppermute | solution.py:89
  24.2 9.9 %collective-permute-start.2 = (f32[192,440]{1,0:T(8,128)S(1)}, f32[192,440]{1,0:T(8,128)S(1)}, u32[]{:S(2)}, u32[]{:S(2)}) collective-permute-start(f32[192,440]{1,0:T(8,128)S(1)} %collective-permute-done.1.refs_4_), channel_id=1, source_target_pairs={{0,8},{2,10},{4,12},{6,14},{8,0},{10,2},{12,4},{14,6},{16,24},{18,... | collective-permute-start | bytes 1013768 | tf_op jit(solution)/shard_map/ppermute | solution.py:89
  28.6 22.0 %collective-permute-start.8 = (f32[192,440]{1,0:T(8,128)S(1)}, f32[192,440]{1,0:T(8,128)S(1)}, u32[]{:S(2)}, u32[]{:S(2)}) collective-permute-start(f32[192,440]{1,0:T(8,128)S(1)} %collective-permute-done.1.refs_4_), channel_id=1, source_target_pairs={{0,2},{2,0},{4,6},{6,4},{8,10},{10,8},{12,14},{14,12},{16,18},{18,... | collective-permute-start | bytes 1013768 | tf_op jit(solution)/shard_map/ppermute | solution.py:89
  30.1 20.9 %collective-permute-start.15 = (f32[192,440]{1,0:T(8,128)S(1)}, f32[192,440]{1,0:T(8,128)S(1)}, u32[]{:S(2)}, u32[]{:S(2)}) collective-permute-start(f32[192,440]{1,0:T(8,128)S(1)} %collective-permute-done.refs_0_), channel_id=1, source_target_pairs={{0,2},{2,0},{4,6},{6,4},{8,10},{10,8},{12,14},{14,12},{16,18},{18,... | collective-permute-start | bytes 1013768 | tf_op jit(solution)/shard_map/ppermute | solution.py:89
  32.8 18.5 %collective-permute-start.9 = (f32[192,440]{1,0:T(8,128)S(1)}, f32[192,440]{1,0:T(8,128)S(1)}, u32[]{:S(2)}, u32[]{:S(2)}) collective-permute-start(f32[192,440]{1,0:T(8,128)S(1)} %collective-permute-done.refs_0_), channel_id=1, source_target_pairs={{0,4},{2,6},{4,0},{6,2},{8,12},{10,14},{12,8},{14,10},{16,20},{18,... | collective-permute-start | bytes 1013768 | tf_op jit(solution)/shard_map/ppermute | solution.py:89
  34.1 18.9 %collective-permute-start.10 = (f32[192,440]{1,0:T(8,128)S(1)}, f32[192,440]{1,0:T(8,128)S(1)}, u32[]{:S(2)}, u32[]{:S(2)}) collective-permute-start(f32[192,440]{1,0:T(8,128)S(1)} %collective-permute-done.4.refs_3_), channel_id=1, source_target_pairs={{0,8},{2,10},{4,12},{6,14},{8,0},{10,2},{12,4},{14,6},{16,24},{18,... | collective-permute-start | bytes 1013768 | tf_op jit(solution)/shard_map/ppermute | solution.py:89
  49.0 16.2 %collective-permute-start.13 = (f32[192,440]{1,0:T(8,128)S(1)}, f32[192,440]{1,0:T(8,128)S(1)}, u32[]{:S(2)}, u32[]{:S(2)}) collective-permute-start(f32[192,440]{1,0:T(8,128)S(1)} %collective-permute-done.3.refs_2_), channel_id=1, source_target_pairs={{0,2},{2,0},{4,6},{6,4},{8,10},{10,8},{12,14},{14,12},{16,18},{18,... | collective-permute-start | bytes 1013768 | tf_op jit(solution)/shard_map/ppermute | solution.py:89
  50.5 15.3 %collective-permute-start.6 = (f32[152,384]{1,0:T(8,128)S(1)}, f32[152,384]{1,0:T(8,128)S(1)}, u32[]{:S(2)}, u32[]{:S(2)}) collective-permute-start(f32[152,384]{1,0:T(8,128)S(1)} %get-tuple-element.45), channel_id=1, source_target_pairs={{0,4},{2,6},{4,0},{6,2},{8,12},{10,14},{12,8},{14,10},{16,20},{18,... | collective-permute-start | bytes 700424 | tf_op jit(solution)/shard_map/ppermute | solution.py:371
  51.0 15.2 %collective-permute-start.5 = (f32[152,384]{1,0:T(8,128)S(1)}, f32[152,384]{1,0:T(8,128)S(1)}, u32[]{:S(2)}, u32[]{:S(2)}) collective-permute-start(f32[152,384]{1,0:T(8,128)S(1)} %get-tuple-element.44.refs_9_), channel_id=1, source_target_pairs={{0,8},{2,10},{4,12},{6,14},{8,0},{10,2},{12,4},{14,6},{16,24},{18,... | collective-permute-start | bytes 700424 | tf_op jit(solution)/shard_map/ppermute | solution.py:371
  51.3 16.2 %collective-permute-start.16 = (f32[192,440]{1,0:T(8,128)S(1)}, f32[192,440]{1,0:T(8,128)S(1)}, u32[]{:S(2)}, u32[]{:S(2)}) collective-permute-start(f32[192,440]{1,0:T(8,128)S(1)} %collective-permute-done.8.refs_1_), channel_id=1, source_target_pairs={{0,8},{2,10},{4,12},{6,14},{8,0},{10,2},{12,4},{14,6},{16,24},{18,... | collective-permute-start | bytes 1013768 | tf_op jit(solution)/shard_map/ppermute | solution.py:89
  53.1 16.0 %collective-permute-start.14 = (f32[192,440]{1,0:T(8,128)S(1)}, f32[192,440]{1,0:T(8,128)S(1)}, u32[]{:S(2)}, u32[]{:S(2)}) collective-permute-start(f32[192,440]{1,0:T(8,128)S(1)} %collective-permute-done.8.refs_1_), channel_id=1, source_target_pairs={{0,4},{2,6},{4,0},{6,2},{8,12},{10,14},{12,8},{14,10},{16,20},{18,... | collective-permute-start | bytes 1013768 | tf_op jit(solution)/shard_map/ppermute | solution.py:89
  65.2 16.2 %collective-permute-start.19 = (f32[192,440]{1,0:T(8,128)S(1)}, f32[192,440]{1,0:T(8,128)S(1)}, u32[]{:S(2)}, u32[]{:S(2)}) collective-permute-start(f32[192,440]{1,0:T(8,128)S(1)} %collective-permute-done.9.refs_2_), channel_id=1, source_target_pairs={{0,2},{2,0},{4,6},{6,4},{8,10},{10,8},{12,14},{14,12},{16,18},{18,... | collective-permute-start | bytes 1013768 | tf_op jit(solution)/shard_map/ppermute | solution.py:89
  65.8 17.1 %collective-permute-start.12 = (f32[152,384]{1,0:T(8,128)S(1)}, f32[152,384]{1,0:T(8,128)S(1)}, u32[]{:S(2)}, u32[]{:S(2)}) collective-permute-start(f32[152,384]{1,0:T(8,128)S(1)} %get-tuple-element.47), channel_id=1, source_target_pairs={{0,12},{2,14},{4,8},{6,10},{8,4},{10,6},{12,0},{14,2},{16,28},{18,... | collective-permute-start | bytes 700424 | tf_op jit(solution)/shard_map/ppermute | solution.py:371
  66.3 16.6 %collective-permute-start.11 = (f32[152,384]{1,0:T(8,128)S(1)}, f32[152,384]{1,0:T(8,128)S(1)}, u32[]{:S(2)}, u32[]{:S(2)}) collective-permute-start(f32[152,384]{1,0:T(8,128)S(1)} %get-tuple-element.46.refs_9_), channel_id=1, source_target_pairs={{0,2},{2,0},{4,6},{6,4},{8,10},{10,8},{12,14},{14,12},{16,18},{18,... | collective-permute-start | bytes 700424 | tf_op jit(solution)/shard_map/ppermute | solution.py:371
  67.5 15.4 %collective-permute-start.20 = (f32[192,440]{1,0:T(8,128)S(1)}, f32[192,440]{1,0:T(8,128)S(1)}, u32[]{:S(2)}, u32[]{:S(2)}) collective-permute-start(f32[192,440]{1,0:T(8,128)S(1)} %collective-permute-done.16.refs_3_), channel_id=1, source_target_pairs={{0,4},{2,6},{4,0},{6,2},{8,12},{10,14},{12,8},{14,10},{16,20},{18,... | collective-permute-start | bytes 1013768 | tf_op jit(solution)/shard_map/ppermute | solution.py:89
  79.6 10.7 %collective-permute-start.18 = (f32[152,384]{1,0:T(8,128)S(1)}, f32[152,384]{1,0:T(8,128)S(1)}, u32[]{:S(2)}, u32[]{:S(2)}) collective-permute-start(f32[152,384]{1,0:T(8,128)S(1)} %get-tuple-element.49), channel_id=1, source_target_pairs={{0,10},{2,8},{4,14},{6,12},{8,2},{10,0},{12,6},{14,4},{16,26},{18,... | collective-permute-start | bytes 700424 | tf_op jit(solution)/shard_map/ppermute | solution.py:371
  81.4 10.4 %collective-permute-start.17 = (f32[152,384]{1,0:T(8,128)S(1)}, f32[152,384]{1,0:T(8,128)S(1)}, u32[]{:S(2)}, u32[]{:S(2)}) collective-permute-start(f32[152,384]{1,0:T(8,128)S(1)} %get-tuple-element.48.refs_7_), channel_id=1, source_target_pairs={{0,6},{2,4},{4,2},{6,0},{8,14},{10,12},{12,10},{14,8},{16,22},{18,... | collective-permute-start | bytes 700424 | tf_op jit(solution)/shard_map/ppermute | solution.py:371
  97.2 10.7 %collective-permute-start.22 = (f32[152,384]{1,0:T(8,128)S(1)}, f32[152,384]{1,0:T(8,128)S(1)}, u32[]{:S(2)}, u32[]{:S(2)}) collective-permute-start(f32[152,384]{1,0:T(8,128)S(1)} %fusion.6.mine), channel_id=1, source_target_pairs={{0,16},{2,18},{4,20},{6,22},{8,24},{10,26},{12,28},{14,30},{16,0},... | collective-permute-start | bytes 700424 | tf_op jit(solution)/shard_map/ppermute | solution.py:89
  108.2 9.6 %collective-permute-start.26 = (f32[152,384]{1,0:T(8,128)S(1)}, f32[152,384]{1,0:T(8,128)S(1)}, u32[]{:S(2)}, u32[]{:S(2)}) collective-permute-start(f32[152,384]{1,0:T(8,128)S(1)} %residual.2.refs_0_.refs_2_), channel_id=1, source_target_pairs={{0,4},{2,6},{4,0},{6,2},{8,12},{10,14},{12,8},{14,10},{16,20},{18,... | collective-permute-start | bytes 700424 | tf_op jit(solution)/shard_map/ppermute | solution.py:89
  114.9 8.5 %collective-permute-start.28 = (f32[152,384]{1,0:T(8,128)S(1)}, f32[152,384]{1,0:T(8,128)S(1)}, u32[]{:S(2)}, u32[]{:S(2)}) collective-permute-start(f32[152,384]{1,0:T(8,128)S(1)} %residual.2.refs_0_.refs_2_), channel_id=1, source_target_pairs={{0,2},{2,0},{4,6},{6,4},{8,10},{10,8},{12,14},{14,12},{16,18},{18,... | collective-permute-start | bytes 700424 | tf_op jit(solution)/shard_map/ppermute | solution.py:89
  149.7 9.2 %collective-permute-start.37 = (f32[152,384]{1,0:T(8,128)S(1)}, f32[152,384]{1,0:T(8,128)S(1)}, u32[]{:S(2)}, u32[]{:S(2)}) collective-permute-start(f32[152,384]{1,0:T(8,128)S(1)} %get-tuple-element.65._), channel_id=1, source_target_pairs={{0,2},{2,0},{4,6},{6,4},{8,10},{10,8},{12,14},{14,12},{16,18},{18,... | collective-permute-start | bytes 700424 | tf_op jit(solution)/shard_map/ppermute | solution.py:89
  154.1 8.7 %collective-permute-start.33 = (f32[152,384]{1,0:T(8,128)S(1)}, f32[152,384]{1,0:T(8,128)S(1)}, u32[]{:S(2)}, u32[]{:S(2)}) collective-permute-start(f32[152,384]{1,0:T(8,128)S(1)} %add.57), channel_id=1, source_target_pairs={{0,2},{2,0},{4,6},{6,4},{8,10},{10,8},{12,14},{14,12},{16,18},{18,... | collective-permute-start | bytes 700424 | tf_op jit(solution)/shard_map/ppermute | solution.py:89
  155.3 10.7 %collective-permute-start.36 = (f32[152,384]{1,0:T(8,128)S(1)}, f32[152,384]{1,0:T(8,128)S(1)}, u32[]{:S(2)}, u32[]{:S(2)}) collective-permute-start(f32[152,384]{1,0:T(8,128)S(1)} %get-tuple-element.66._), channel_id=1, source_target_pairs={{0,2},{2,0},{4,6},{6,4},{8,10},{10,8},{12,14},{14,12},{16,18},{18,... | collective-permute-start | bytes 700424 | tf_op jit(solution)/shard_map/ppermute | solution.py:89
  169.8 9.1 %collective-permute-start.39 = (f32[152,384]{1,0:T(8,128)S(1)}, f32[152,384]{1,0:T(8,128)S(1)}, u32[]{:S(2)}, u32[]{:S(2)}) collective-permute-start(f32[152,384]{1,0:T(8,128)S(1)} %fusion.8.mine), channel_id=1, source_target_pairs={{0,16},{2,18},{4,20},{6,22},{8,24},{10,26},{12,28},{14,30},{16,0},... | collective-permute-start | bytes 700424 | tf_op jit(solution)/shard_map/ppermute | solution.py:89
  179.2 10.5 %collective-permute-start.43 = (f32[152,384]{1,0:T(8,128)S(1)}, f32[152,384]{1,0:T(8,128)S(1)}, u32[]{:S(2)}, u32[]{:S(2)}) collective-permute-start(f32[152,384]{1,0:T(8,128)S(1)} %residual.3.refs_0_.refs_2_), channel_id=1, source_target_pairs={{0,4},{2,6},{4,0},{6,2},{8,12},{10,14},{12,8},{14,10},{16,20},{18,... | collective-permute-start | bytes 700424 | tf_op jit(solution)/shard_map/ppermute | solution.py:89
  186.7 9.1 %collective-permute-start.45 = (f32[152,384]{1,0:T(8,128)S(1)}, f32[152,384]{1,0:T(8,128)S(1)}, u32[]{:S(2)}, u32[]{:S(2)}) collective-permute-start(f32[152,384]{1,0:T(8,128)S(1)} %residual.3.refs_0_.refs_2_), channel_id=1, source_target_pairs={{0,2},{2,0},{4,6},{6,4},{8,10},{10,8},{12,14},{14,12},{16,18},{18,... | collective-permute-start | bytes 700424 | tf_op jit(solution)/shard_map/ppermute | solution.py:89
  187.3 8.5 %collective-permute-start.46 = (f32[152,384]{1,0:T(8,128)S(1)}, f32[152,384]{1,0:T(8,128)S(1)}, u32[]{:S(2)}, u32[]{:S(2)}) collective-permute-start(f32[152,384]{1,0:T(8,128)S(1)} %collective-permute-done.40.refs_0_), channel_id=1, source_target_pairs={{0,4},{2,6},{4,0},{6,2},{8,12},{10,14},{12,8},{14,10},{16,20},{18,... | collective-permute-start | bytes 700424 | tf_op jit(solution)/shard_map/ppermute | solution.py:89
  189.8 8.6 %collective-permute-start.44 = (f32[152,384]{1,0:T(8,128)S(1)}, f32[152,384]{1,0:T(8,128)S(1)}, u32[]{:S(2)}, u32[]{:S(2)}) collective-permute-start(f32[152,384]{1,0:T(8,128)S(1)} %collective-permute-done.43.refs_1_), channel_id=1, source_target_pairs={{0,2},{2,0},{4,6},{6,4},{8,10},{10,8},{12,14},{14,12},{16,18},{18,... | collective-permute-start | bytes 700424 | tf_op jit(solution)/shard_map/ppermute | solution.py:89
  (23 other events, 157.5 us)

commit v2 on v1

--- a/solution.py
+++ b/solution.py
@@ -173,7 +173,7 @@
         scratch_shapes=[pltpu.VMEM((2, count, depth), BF16), pltpu.VMEM((rows, count), F32)],
         compiler_params=pltpu.CompilerParams(vmem_limit_bytes=VMEM_FEATURES),
         cost_estimate=pl.CostEstimate(
-            flops=6 * count * feats * (depth + rows), bytes_accessed=4 * count * feats, transcendentals=0
+            flops=8 * count * feats * (depth + rows), bytes_accessed=4 * count * feats, transcendentals=0
         ),
         name="features",
     )(*frames, *proj, phase, *look, *after)
@@ -196,7 +196,7 @@
         out_shape=[jax.ShapeDtypeStruct((rows, columns), F32) for columns in widths],
         compiler_params=pltpu.CompilerParams(vmem_limit_bytes=VMEM_PRODUCTS),
         cost_estimate=pl.CostEstimate(
-            flops=6 * count * feats * rows, bytes_accessed=4 * count * feats, transcendentals=0
+            flops=8 * count * feats * rows, bytes_accessed=4 * count * feats, transcendentals=0
         ),
         name="scores",
     )(*look, high, low, after)
@@ -244,7 +244,7 @@
         scratch_shapes=[pltpu.VMEM((2 * rows, count), BF16)],
         compiler_params=pltpu.CompilerParams(vmem_limit_bytes=VMEM_PRODUCTS),
         cost_estimate=pl.CostEstimate(
-            flops=6 * count * feats * rows, bytes_accessed=4 * count * feats, transcendentals=0
+            flops=8 * count * feats * rows, bytes_accessed=4 * count * feats, transcendentals=0
         ),
         name="gradient",
     )(*residual, high, low, *([] if first else [before]))

time: 217 us -> 216 us (level)
  transfers between devices with their start and end apart: 49 -> 49, of which waited for: 20 -> 19; matrix products, arithmetic and copies ran while one was open for 2% -> 2% of each run, Pallas kernels for 32% -> 32%
where the time goes in v2:
time: 216 us; the launch traced here: 215 us
  Pallas kernels  75.1 us (35%)
  starting transfers between devices  56.9 us (26%)
  waiting for transfers between devices  53.2 us (25%)
  blocking collectives  22.3 us (10%)
  local copies, waits for them, and re-layouts  3.46 us (2%)
  other arithmetic  3.3 us (2%)
    ppermute x42, starting transfers between devices, swap(): return lax.ppermute(value, axis, [(i, i ^ 1 << bit) for i in range(count)])  50 us
    ppermute x42, waiting for transfers between devices, swap(): return lax.ppermute(value, axis, [(i, i ^ 1 << bit) for i in range(count)])  46.5 us
    pallas_call x5, Pallas kernels, features_call(): pl.pallas_call(functools.partial(features_kernel, arrays=len(frames), aft...  44.1 us
    all_to_all x2, blocking collectives, on_device(): tiles = lax.all_to_all(tiles, 'feat', 0, 0)  22.3 us
    pallas_call x12, Pallas kernels, gradient_call(): pl.pallas_call(functools.partial(gradient_kernel, halves=halves, first=fi...  17.9 us
    pallas_call x5, Pallas kernels, scores_call(): pl.pallas_call(scores_kernel, in_specs=[whole] * 4 + [pl.BlockSpec(memory...  8.71 us
    ppermute x7, starting transfers between devices, first_scores(): lax.ppermute(value, 'feat', [(i, i ^ unit) for i in range(count)])  6.93 us
    ppermute x7, waiting for transfers between devices, first_scores(): lax.ppermute(value, 'feat', [(i, i ^ unit) for i in range(count)])  6.72 us
  transfers between devices with their start and end apart: 49, of which 19 were waited for; matrix products, arithmetic and copies ran while one was open for 2% of the time, Pallas kernels for 32%

profile of v2, /device:TPU:0, one launch (start us, length us, event | category | flops | bytes accessed | tf_op | source)
XLA Modules:
  0.0 215.4 jit_solution(17210809656021541785)
XLA Ops:
  0.6 4.1 %collective-permute-start.1 = (f32[192,440]{1,0:T(8,128)}, f32[192,440]{1,0:T(8,128)S(1)}, u32[]{:S(2)}, u32[]{:S(2)}) collective-permute-start(f32[192,440]{1,0:T(8,128)} %refs_0_.1), channel_id=1, source_target_pairs={{0,16},{2,18},{4,20},{6,22},{8,24},{10,26},{12,28},{14,30},{16,0},... | collective-permute-start | bytes 1013768 | tf_op jit(solution)/shard_map/ppermute | solution.py:89
  13.2 2.8 %fusion = (bf16[440,2048]{1,0:T(8,128)(2,1)S(1)}, bf16[440,2048]{1,0:T(8,128)(2,1)S(1)}) fusion(f32[440,2048]{1,0:T(8,128)} %param.8), kind=kLoop, calls=%fused_computation.2 | loop fusion | flops 4505600 | bytes 7208960 | tf_op jit(solution)/shard_map/convert_element_type | solution.py:45
  16.1 6.5 %collective-permute-done.1.refs_4_ = f32[192,440]{1,0:T(8,128)S(1)} collective-permute-done((f32[192,440]{1,0:T(8,128)}, f32[192,440]{1,0:T(8,128)S(1)}, u32[]{:S(2)}, u32[]{:S(2)}) %collective-permute-start.1) | collective-permute-done | bytes 337952 | tf_op jit(solution)/shard_map/ppermute | solution.py:89
  24.8 3.7 %features.5 = (bf16[192,2048]{1,0:T(8,128)(2,1)S(1)}, bf16[192,2048]{1,0:T(8,128)(2,1)S(1)}, f32[152,192]{1,0:T(8,128)S(1)}) custom-call(f32[192,440]{1,0:T(8,128)S(1)} %copy-done.4, bf16[440,2048]{1,0:T(8,128)(2,1)S(1)} %get-tuple-element.79.refs_1_.refs_5_.refs_4_.refs_2_, bf16[440,2048]{1,0:T(8,128)(2,1)S(1)} %get-tuple-element.78.refs_2_.refs_6_.refs_5_.refs_3_, ...), custom_call_target="tpu_custom_call" | custom-call | flops 1862270976 | bytes 1572864 | tf_op jit(solution)/shard_map/features/pallas_call | solution.py:167
  30.7 2.2 %collective-permute-done.4.refs_3_ = f32[192,440]{1,0:T(8,128)S(1)} collective-permute-done((f32[192,440]{1,0:T(8,128)S(1)}, f32[192,440]{1,0:T(8,128)S(1)}, u32[]{:S(2)}, u32[]{:S(2)}) %collective-permute-start.4) | collective-permute-done | bytes 337952 | tf_op jit(solution)/shard_map/ppermute | solution.py:89
  34.1 1.8 collective-permute-start.10
  35.9 13.1 %features.6 = (bf16[960,2048]{1,0:T(8,128)(2,1)S(1)}, bf16[960,2048]{1,0:T(8,128)(2,1)S(1)}, f32[152,384]{1,0:T(8,128)S(1)}, f32[152,384]{1,0:T(8,128)S(1)}, f32[152,192]{1,0:T(8,128)S(1)}) custom-call(f32[192,440]{1,0:T(8,128)S(1)} %collective-permute-done.refs_0_, f32[192,440]{1,0:T(8,128)S(1)} %collective-permute-done.2.refs_1_, ...), custom_call_target="tpu_custom_call" | custom-call | flops 9311354880 | bytes 7864320 | tf_op jit(solution)/shard_map/features/pallas_call | solution.py:167
  54.6 10.6 %features.7 = (bf16[768,2048]{1,0:T(8,128)(2,1)S(1)}, bf16[768,2048]{1,0:T(8,128)(2,1)S(1)}, f32[152,384]{1,0:T(8,128)S(1)}, f32[152,384]{1,0:T(8,128)S(1)}) custom-call(f32[192,440]{1,0:T(8,128)S(1)} %collective-permute-done.7.refs_0_, f32[192,440]{1,0:T(8,128)S(1)} %collective-permute-done.8.refs_1_, f32[192,440]{1,0:T(8,128)S(1)} %collective-permute-done.9.refs_2_, ...), custom_call_target="tpu_custom_call" | custom-call | flops 7449083904 | bytes 6291456 | tf_op jit(solution)/shard_map/features/pallas_call | solution.py:167
  69.0 10.6 %features.8 = (bf16[768,2048]{1,0:T(8,128)(2,1)S(1)}, bf16[768,2048]{1,0:T(8,128)(2,1)S(1)}, f32[152,384]{1,0:T(8,128)S(1)}, f32[152,384]{1,0:T(8,128)S(1)}) custom-call(f32[192,440]{1,0:T(8,128)S(1)} %collective-permute-done.13.refs_0_, f32[192,440]{1,0:T(8,128)S(1)} %collective-permute-done.14.refs_1_, f32[192,440]{1,0:T(8,128)S(1)} %collective-permute-done.15.refs_2_, ...), custom_call_target="tpu_custom_call" | custom-call | flops 7449083904 | bytes 6291456 | tf_op jit(solution)/shard_map/features/pallas_call | solution.py:167
  79.6 1.8 collective-permute-start.18
  82.8 6.1 %features.9 = (bf16[384,2048]{1,0:T(8,128)(2,1)S(1)}, bf16[384,2048]{1,0:T(8,128)(2,1)S(1)}, f32[152,384]{1,0:T(8,128)S(1)}) custom-call(f32[192,440]{1,0:T(8,128)S(1)} %collective-permute-done.19.refs_0_, f32[192,440]{1,0:T(8,128)S(1)} %collective-permute-done.20.refs_1_, bf16[440,2048]{1,0:T(8,128)(2,1)S(1)} %get-tuple-element.79.refs_1_.refs_5_.refs_4_.refs_2_, ...), custom_call_target="tpu_custom_call" | custom-call | flops 3724541952 | bytes 3145728 | tf_op jit(solution)/shard_map/features/pallas_call | solution.py:167
  91.9 5.1 %collective-permute-done.21 = f32[152,384]{1,0:T(8,128)S(1)} collective-permute-done((f32[152,384]{1,0:T(8,128)S(1)}, f32[152,384]{1,0:T(8,128)S(1)}, u32[]{:S(2)}, u32[]{:S(2)}) %collective-permute-start.21) | collective-permute-done | bytes 233504 | tf_op jit(solution)/shard_map/ppermute | solution.py:371
  97.1 5.3 %collective-permute-start.22 = (f32[152,384]{1,0:T(8,128)S(1)}, f32[152,384]{1,0:T(8,128)S(1)}, u32[]{:S(2)}, u32[]{:S(2)}) collective-permute-start(f32[152,384]{1,0:T(8,128)S(1)} %fusion.6.mine), channel_id=1, source_target_pairs={{0,16},{2,18},{4,20},{6,22},{8,24},{10,26},{12,28},{14,30},{16,0},... | collective-permute-start | bytes 700424 | tf_op jit(solution)/shard_map/ppermute | solution.py:89
  102.4 5.4 %collective-permute-done.22.theirs = f32[152,384]{1,0:T(8,128)S(1)} collective-permute-done((f32[152,384]{1,0:T(8,128)S(1)}, f32[152,384]{1,0:T(8,128)S(1)}, u32[]{:S(2)}, u32[]{:S(2)}) %collective-permute-start.22) | collective-permute-done | bytes 233504 | tf_op jit(solution)/shard_map/ppermute | solution.py:89
  110.2 4.0 %collective-permute-done.23.refs_0_ = f32[152,384]{1,0:T(8,128)S(1)} collective-permute-done((f32[152,384]{1,0:T(8,128)S(1)}, f32[152,384]{1,0:T(8,128)S(1)}, u32[]{:S(2)}, u32[]{:S(2)}) %collective-permute-start.23) | collective-permute-done | bytes 233504 | tf_op jit(solution)/shard_map/ppermute | solution.py:89
  117.8 2.7 %gradient.13.refs_4_ = f32[152,2048]{1,0:T(8,128)S(1)} custom-call(f32[152,384]{1,0:T(8,128)S(1)} %collective-permute-done.23.refs_0_, f32[152,384]{1,0:T(8,128)S(1)} %collective-permute-done.26.refs_1_, f32[152,384]{1,0:T(8,128)S(1)} %residual.2.refs_0_.refs_2_, ...), custom_call_target="tpu_custom_call", output_to_operand_aliasing={{}: (5, {})} | custom-call | flops 2390753280 | bytes 7864320 | tf_op jit(solution)/shard_map/gradient/pallas_call | solution.py:238
  122.6 2.0 gradient.14.refs_4_
  124.6 2.0 gradient.15.refs_3_
  132.3 11.2 %all_to_all.10.tiles = f32[16,8,128]{2,1,0:T(8,128)S(1)} all-to-all(f32[16,8,128]{2,1,0:T(8,128)S(1)} %get-tuple-element.61), channel_id=1, replica_groups=mesh['feat'=16,'frame'=2] {'feat'}, dimensions={0} | all-to-all | bytes 131072 | tf_op jit(solution)/shard_map/all_to_all | solution.py:424
  146.5 2.0 scores.6
  149.1 2.0 scores.7
  155.0 2.7 %scores.8 = (f32[152,384]{1,0:T(8,128)S(1)}, f32[152,384]{1,0:T(8,128)S(1)}, f32[152,192]{1,0:T(8,128)S(1)}) custom-call(bf16[304,2048]{1,0:T(8,128)(2,1)S(1)} %get-tuple-element.63.look, bf16[152,2048]{1,0:T(8,128)(2,1)S(1)} %get-tuple-element.64.look_high._, bf16[960,2048]{1,0:T(8,128)(2,1)S(1)} %get-tuple-element.57.refs_3_.high, ...), custom_call_target="tpu_custom_call" | custom-call | flops 2390753280 | bytes 7864320 | tf_op jit(solution)/shard_map/scores/pallas_call | solution.py:192
  158.3 3.3 %collective-permute-done.33 = f32[152,384]{1,0:T(8,128)S(1)} collective-permute-done((f32[152,384]{1,0:T(8,128)S(1)}, f32[152,384]{1,0:T(8,128)S(1)}, u32[]{:S(2)}, u32[]{:S(2)}) %collective-permute-start.33) | collective-permute-done | bytes 233504 | tf_op jit(solution)/shard_map/ppermute | solution.py:89
  162.8 2.1 collective-permute-done.36
  164.8 3.7 %collective-permute-done.35 = f32[152,384]{1,0:T(8,128)S(1)} collective-permute-done((f32[152,384]{1,0:T(8,128)S(1)}, f32[152,384]{1,0:T(8,128)S(1)}, u32[]{:S(2)}, u32[]{:S(2)}) %collective-permute-start.35) | collective-permute-done | bytes 233504 | tf_op jit(solution)/shard_map/ppermute | solution.py:89
  168.7 9.0 %collective-permute-done.39.theirs = f32[152,384]{1,0:T(8,128)S(1)} collective-permute-done((f32[152,384]{1,0:T(8,128)S(1)}, f32[152,384]{1,0:T(8,128)S(1)}, u32[]{:S(2)}, u32[]{:S(2)}) %collective-permute-start.39) | collective-permute-done | bytes 233504 | tf_op jit(solution)/shard_map/ppermute | solution.py:89
  178.1 3.6 %collective-permute-start.43 = (f32[152,384]{1,0:T(8,128)S(1)}, f32[152,384]{1,0:T(8,128)S(1)}, u32[]{:S(2)}, u32[]{:S(2)}) collective-permute-start(f32[152,384]{1,0:T(8,128)S(1)} %residual.3.refs_0_.refs_2_), channel_id=1, source_target_pairs={{0,4},{2,6},{4,0},{6,2},{8,12},{10,14},{12,8},{14,10},{16,20},{18,... | collective-permute-start | bytes 700424 | tf_op jit(solution)/shard_map/ppermute | solution.py:89
  181.7 2.4 %collective-permute-done.40.refs_0_ = f32[152,384]{1,0:T(8,128)S(1)} collective-permute-done((f32[152,384]{1,0:T(8,128)S(1)}, f32[152,384]{1,0:T(8,128)S(1)}, u32[]{:S(2)}, u32[]{:S(2)}) %collective-permute-start.40) | collective-permute-done | bytes 233504 | tf_op jit(solution)/shard_map/ppermute | solution.py:89
  188.7 2.6 %gradient.19.refs_4_ = f32[152,2048]{1,0:T(8,128)S(1)} custom-call(f32[152,384]{1,0:T(8,128)S(1)} %collective-permute-done.40.refs_0_, f32[152,384]{1,0:T(8,128)S(1)} %collective-permute-done.43.refs_1_, f32[152,384]{1,0:T(8,128)S(1)} %residual.3.refs_0_.refs_2_, ...), custom_call_target="tpu_custom_call", output_to_operand_aliasing={{}: (5, {})} | custom-call | flops 2390753280 | bytes 7864320 | tf_op jit(solution)/shard_map/gradient/pallas_call | solution.py:238
  193.9 2.0 gradient.20.refs_4_
  195.9 2.2 %gradient.21.refs_3_ = f32[152,2048]{1,0:T(8,128)S(1)} custom-call(f32[152,384]{1,0:T(8,128)S(1)} %collective-permute-done.44.refs_0_, f32[152,384]{1,0:T(8,128)S(1)} %collective-permute-done.41.refs_1_, bf16[768,2048]{1,0:T(8,128)(2,1)S(1)} %get-tuple-element.53.refs_2_.high, ...), custom_call_target="tpu_custom_call", output_to_operand_aliasing={{}: (4, {})} | custom-call | flops 1912602624 | bytes 6291456 | tf_op jit(solution)/shard_map/gradient/pallas_call | solution.py:238
  202.5 11.1 %all_to_all.11.tiles = f32[16,8,128]{2,1,0:T(8,128)S(1)} all-to-all(f32[16,8,128]{2,1,0:T(8,128)S(1)} %get-tuple-element.72), channel_id=1, replica_groups=mesh['feat'=16,'frame'=2] {'feat'}, dimensions={0} | all-to-all | bytes 131072 | tf_op jit(solution)/shard_map/all_to_all | solution.py:424
  (119 shorter events, 64.7 us)
Async XLA Ops:
  0.6 22.0 %collective-permute-start.1 = (f32[192,440]{1,0:T(8,128)}, f32[192,440]{1,0:T(8,128)S(1)}, u32[]{:S(2)}, u32[]{:S(2)}) collective-permute-start(f32[192,440]{1,0:T(8,128)} %refs_0_.1), channel_id=1, source_target_pairs={{0,16},{2,18},{4,20},{6,22},{8,24},{10,26},{12,28},{14,30},{16,0},... | collective-permute-start | bytes 1013768 | tf_op jit(solution)/shard_map/ppermute | solution.py:89
  4.7 23.8 %collective-permute-start = (f32[192,440]{1,0:T(8,128)}, f32[192,440]{1,0:T(8,128)S(1)}, u32[]{:S(2)}, u32[]{:S(2)}) collective-permute-start(f32[192,440]{1,0:T(8,128)} %refs_0_.1), channel_id=1, source_target_pairs={{0,8},{2,10},{4,12},{6,14},{8,0},{10,2},{12,4},{14,6},{16,24},{18,... | collective-permute-start | bytes 1013768 | tf_op jit(solution)/shard_map/ppermute | solution.py:89
  6.3 42.6 %collective-permute-start.7 = (f32[192,440]{1,0:T(8,128)}, f32[192,440]{1,0:T(8,128)S(1)}, u32[]{:S(2)}, u32[]{:S(2)}) collective-permute-start(f32[192,440]{1,0:T(8,128)} %refs_0_.1), channel_id=1, source_target_pairs={{0,2},{2,0},{4,6},{6,4},{8,10},{10,8},{12,14},{14,12},{16,18},{18,... | collective-permute-start | bytes 1013768 | tf_op jit(solution)/shard_map/ppermute | solution.py:89
  7.8 22.3 %collective-permute-start.3 = (f32[192,440]{1,0:T(8,128)}, f32[192,440]{1,0:T(8,128)S(1)}, u32[]{:S(2)}, u32[]{:S(2)}) collective-permute-start(f32[192,440]{1,0:T(8,128)} %refs_0_.1), channel_id=1, source_target_pairs={{0,4},{2,6},{4,0},{6,2},{8,12},{10,14},{12,8},{14,10},{16,20},{18,... | collective-permute-start | bytes 1013768 | tf_op jit(solution)/shard_map/ppermute | solution.py:89
  22.6 10.2 %collective-permute-start.4 = (f32[192,440]{1,0:T(8,128)S(1)}, f32[192,440]{1,0:T(8,128)S(1)}, u32[]{:S(2)}, u32[]{:S(2)}) collective-permute-start(f32[192,440]{1,0:T(8,128)S(1)} %collective-permute-done.1.refs_4_), channel_id=1, source_target_pairs={{0,4},{2,6},{4,0},{6,2},{8,12},{10,14},{12,8},{14,10},{16,20},{18,... | collective-permute-start | bytes 1013768 | tf_op jit(solution)/shard_map/ppermute | solution.py:89
  24.2 9.9 %collective-permute-start.2 = (f32[192,440]{1,0:T(8,128)S(1)}, f32[192,440]{1,0:T(8,128)S(1)}, u32[]{:S(2)}, u32[]{:S(2)}) collective-permute-start(f32[192,440]{1,0:T(8,128)S(1)} %collective-permute-done.1.refs_4_), channel_id=1, source_target_pairs={{0,8},{2,10},{4,12},{6,14},{8,0},{10,2},{12,4},{14,6},{16,24},{18,... | collective-permute-start | bytes 1013768 | tf_op jit(solution)/shard_map/ppermute | solution.py:89
  28.6 21.9 %collective-permute-start.8 = (f32[192,440]{1,0:T(8,128)S(1)}, f32[192,440]{1,0:T(8,128)S(1)}, u32[]{:S(2)}, u32[]{:S(2)}) collective-permute-start(f32[192,440]{1,0:T(8,128)S(1)} %collective-permute-done.1.refs_4_), channel_id=1, source_target_pairs={{0,2},{2,0},{4,6},{6,4},{8,10},{10,8},{12,14},{14,12},{16,18},{18,... | collective-permute-start | bytes 1013768 | tf_op jit(solution)/shard_map/ppermute | solution.py:89
  30.1 20.9 %collective-permute-start.15 = (f32[192,440]{1,0:T(8,128)S(1)}, f32[192,440]{1,0:T(8,128)S(1)}, u32[]{:S(2)}, u32[]{:S(2)}) collective-permute-start(f32[192,440]{1,0:T(8,128)S(1)} %collective-permute-done.refs_0_), channel_id=1, source_target_pairs={{0,2},{2,0},{4,6},{6,4},{8,10},{10,8},{12,14},{14,12},{16,18},{18,... | collective-permute-start | bytes 1013768 | tf_op jit(solution)/shard_map/ppermute | solution.py:89
  32.8 18.4 %collective-permute-start.9 = (f32[192,440]{1,0:T(8,128)S(1)}, f32[192,440]{1,0:T(8,128)S(1)}, u32[]{:S(2)}, u32[]{:S(2)}) collective-permute-start(f32[192,440]{1,0:T(8,128)S(1)} %collective-permute-done.refs_0_), channel_id=1, source_target_pairs={{0,4},{2,6},{4,0},{6,2},{8,12},{10,14},{12,8},{14,10},{16,20},{18,... | collective-permute-start | bytes 1013768 | tf_op jit(solution)/shard_map/ppermute | solution.py:89
  34.1 18.9 %collective-permute-start.10 = (f32[192,440]{1,0:T(8,128)S(1)}, f32[192,440]{1,0:T(8,128)S(1)}, u32[]{:S(2)}, u32[]{:S(2)}) collective-permute-start(f32[192,440]{1,0:T(8,128)S(1)} %collective-permute-done.4.refs_3_), channel_id=1, source_target_pairs={{0,8},{2,10},{4,12},{6,14},{8,0},{10,2},{12,4},{14,6},{16,24},{18,... | collective-permute-start | bytes 1013768 | tf_op jit(solution)/shard_map/ppermute | solution.py:89
  49.0 16.2 %collective-permute-start.13 = (f32[192,440]{1,0:T(8,128)S(1)}, f32[192,440]{1,0:T(8,128)S(1)}, u32[]{:S(2)}, u32[]{:S(2)}) collective-permute-start(f32[192,440]{1,0:T(8,128)S(1)} %collective-permute-done.3.refs_2_), channel_id=1, source_target_pairs={{0,2},{2,0},{4,6},{6,4},{8,10},{10,8},{12,14},{14,12},{16,18},{18,... | collective-permute-start | bytes 1013768 | tf_op jit(solution)/shard_map/ppermute | solution.py:89
  50.5 15.3 %collective-permute-start.6 = (f32[152,384]{1,0:T(8,128)S(1)}, f32[152,384]{1,0:T(8,128)S(1)}, u32[]{:S(2)}, u32[]{:S(2)}) collective-permute-start(f32[152,384]{1,0:T(8,128)S(1)} %get-tuple-element.45), channel_id=1, source_target_pairs={{0,4},{2,6},{4,0},{6,2},{8,12},{10,14},{12,8},{14,10},{16,20},{18,... | collective-permute-start | bytes 700424 | tf_op jit(solution)/shard_map/ppermute | solution.py:371
  51.0 15.2 %collective-permute-start.5 = (f32[152,384]{1,0:T(8,128)S(1)}, f32[152,384]{1,0:T(8,128)S(1)}, u32[]{:S(2)}, u32[]{:S(2)}) collective-permute-start(f32[152,384]{1,0:T(8,128)S(1)} %get-tuple-element.44.refs_9_), channel_id=1, source_target_pairs={{0,8},{2,10},{4,12},{6,14},{8,0},{10,2},{12,4},{14,6},{16,24},{18,... | collective-permute-start | bytes 700424 | tf_op jit(solution)/shard_map/ppermute | solution.py:371
  51.3 16.2 %collective-permute-start.16 = (f32[192,440]{1,0:T(8,128)S(1)}, f32[192,440]{1,0:T(8,128)S(1)}, u32[]{:S(2)}, u32[]{:S(2)}) collective-permute-start(f32[192,440]{1,0:T(8,128)S(1)} %collective-permute-done.8.refs_1_), channel_id=1, source_target_pairs={{0,8},{2,10},{4,12},{6,14},{8,0},{10,2},{12,4},{14,6},{16,24},{18,... | collective-permute-start | bytes 1013768 | tf_op jit(solution)/shard_map/ppermute | solution.py:89
  53.0 16.0 %collective-permute-start.14 = (f32[192,440]{1,0:T(8,128)S(1)}, f32[192,440]{1,0:T(8,128)S(1)}, u32[]{:S(2)}, u32[]{:S(2)}) collective-permute-start(f32[192,440]{1,0:T(8,128)S(1)} %collective-permute-done.8.refs_1_), channel_id=1, source_target_pairs={{0,4},{2,6},{4,0},{6,2},{8,12},{10,14},{12,8},{14,10},{16,20},{18,... | collective-permute-start | bytes 1013768 | tf_op jit(solution)/shard_map/ppermute | solution.py:89
  65.2 16.2 %collective-permute-start.19 = (f32[192,440]{1,0:T(8,128)S(1)}, f32[192,440]{1,0:T(8,128)S(1)}, u32[]{:S(2)}, u32[]{:S(2)}) collective-permute-start(f32[192,440]{1,0:T(8,128)S(1)} %collective-permute-done.9.refs_2_), channel_id=1, source_target_pairs={{0,2},{2,0},{4,6},{6,4},{8,10},{10,8},{12,14},{14,12},{16,18},{18,... | collective-permute-start | bytes 1013768 | tf_op jit(solution)/shard_map/ppermute | solution.py:89
  65.8 17.0 %collective-permute-start.12 = (f32[152,384]{1,0:T(8,128)S(1)}, f32[152,384]{1,0:T(8,128)S(1)}, u32[]{:S(2)}, u32[]{:S(2)}) collective-permute-start(f32[152,384]{1,0:T(8,128)S(1)} %get-tuple-element.47), channel_id=1, source_target_pairs={{0,12},{2,14},{4,8},{6,10},{8,4},{10,6},{12,0},{14,2},{16,28},{18,... | collective-permute-start | bytes 700424 | tf_op jit(solution)/shard_map/ppermute | solution.py:371
  66.2 16.6 %collective-permute-start.11 = (f32[152,384]{1,0:T(8,128)S(1)}, f32[152,384]{1,0:T(8,128)S(1)}, u32[]{:S(2)}, u32[]{:S(2)}) collective-permute-start(f32[152,384]{1,0:T(8,128)S(1)} %get-tuple-element.46.refs_9_), channel_id=1, source_target_pairs={{0,2},{2,0},{4,6},{6,4},{8,10},{10,8},{12,14},{14,12},{16,18},{18,... | collective-permute-start | bytes 700424 | tf_op jit(solution)/shard_map/ppermute | solution.py:371
  67.5 15.4 %collective-permute-start.20 = (f32[192,440]{1,0:T(8,128)S(1)}, f32[192,440]{1,0:T(8,128)S(1)}, u32[]{:S(2)}, u32[]{:S(2)}) collective-permute-start(f32[192,440]{1,0:T(8,128)S(1)} %collective-permute-done.16.refs_3_), channel_id=1, source_target_pairs={{0,4},{2,6},{4,0},{6,2},{8,12},{10,14},{12,8},{14,10},{16,20},{18,... | collective-permute-start | bytes 1013768 | tf_op jit(solution)/shard_map/ppermute | solution.py:89
  79.6 10.6 %collective-permute-start.18 = (f32[152,384]{1,0:T(8,128)S(1)}, f32[152,384]{1,0:T(8,128)S(1)}, u32[]{:S(2)}, u32[]{:S(2)}) collective-permute-start(f32[152,384]{1,0:T(8,128)S(1)} %get-tuple-element.49), channel_id=1, source_target_pairs={{0,10},{2,8},{4,14},{6,12},{8,2},{10,0},{12,6},{14,4},{16,26},{18,... | collective-permute-start | bytes 700424 | tf_op jit(solution)/shard_map/ppermute | solution.py:371
  81.4 10.5 %collective-permute-start.17 = (f32[152,384]{1,0:T(8,128)S(1)}, f32[152,384]{1,0:T(8,128)S(1)}, u32[]{:S(2)}, u32[]{:S(2)}) collective-permute-start(f32[152,384]{1,0:T(8,128)S(1)} %get-tuple-element.48.refs_7_), channel_id=1, source_target_pairs={{0,6},{2,4},{4,2},{6,0},{8,14},{10,12},{12,10},{14,8},{16,22},{18,... | collective-permute-start | bytes 700424 | tf_op jit(solution)/shard_map/ppermute | solution.py:371
  97.1 10.7 %collective-permute-start.22 = (f32[152,384]{1,0:T(8,128)S(1)}, f32[152,384]{1,0:T(8,128)S(1)}, u32[]{:S(2)}, u32[]{:S(2)}) collective-permute-start(f32[152,384]{1,0:T(8,128)S(1)} %fusion.6.mine), channel_id=1, source_target_pairs={{0,16},{2,18},{4,20},{6,22},{8,24},{10,26},{12,28},{14,30},{16,0},... | collective-permute-start | bytes 700424 | tf_op jit(solution)/shard_map/ppermute | solution.py:89
  108.1 8.9 %collective-permute-start.26 = (f32[152,384]{1,0:T(8,128)S(1)}, f32[152,384]{1,0:T(8,128)S(1)}, u32[]{:S(2)}, u32[]{:S(2)}) collective-permute-start(f32[152,384]{1,0:T(8,128)S(1)} %residual.2.refs_0_.refs_2_), channel_id=1, source_target_pairs={{0,4},{2,6},{4,0},{6,2},{8,12},{10,14},{12,8},{14,10},{16,20},{18,... | collective-permute-start | bytes 700424 | tf_op jit(solution)/shard_map/ppermute | solution.py:89
  108.8 13.8 %collective-permute-start.28 = (f32[152,384]{1,0:T(8,128)S(1)}, f32[152,384]{1,0:T(8,128)S(1)}, u32[]{:S(2)}, u32[]{:S(2)}) collective-permute-start(f32[152,384]{1,0:T(8,128)S(1)} %residual.2.refs_0_.refs_2_), channel_id=1, source_target_pairs={{0,2},{2,0},{4,6},{6,4},{8,10},{10,8},{12,14},{14,12},{16,18},{18,... | collective-permute-start | bytes 700424 | tf_op jit(solution)/shard_map/ppermute | solution.py:89
  148.5 9.2 %collective-permute-start.37 = (f32[152,384]{1,0:T(8,128)S(1)}, f32[152,384]{1,0:T(8,128)S(1)}, u32[]{:S(2)}, u32[]{:S(2)}) collective-permute-start(f32[152,384]{1,0:T(8,128)S(1)} %get-tuple-element.65._), channel_id=1, source_target_pairs={{0,2},{2,0},{4,6},{6,4},{8,10},{10,8},{12,14},{14,12},{16,18},{18,... | collective-permute-start | bytes 700424 | tf_op jit(solution)/shard_map/ppermute | solution.py:89
  152.9 8.7 %collective-permute-start.33 = (f32[152,384]{1,0:T(8,128)S(1)}, f32[152,384]{1,0:T(8,128)S(1)}, u32[]{:S(2)}, u32[]{:S(2)}) collective-permute-start(f32[152,384]{1,0:T(8,128)S(1)} %add.57), channel_id=1, source_target_pairs={{0,2},{2,0},{4,6},{6,4},{8,10},{10,8},{12,14},{14,12},{16,18},{18,... | collective-permute-start | bytes 700424 | tf_op jit(solution)/shard_map/ppermute | solution.py:89
  154.1 10.7 %collective-permute-start.36 = (f32[152,384]{1,0:T(8,128)S(1)}, f32[152,384]{1,0:T(8,128)S(1)}, u32[]{:S(2)}, u32[]{:S(2)}) collective-permute-start(f32[152,384]{1,0:T(8,128)S(1)} %get-tuple-element.66._), channel_id=1, source_target_pairs={{0,2},{2,0},{4,6},{6,4},{8,10},{10,8},{12,14},{14,12},{16,18},{18,... | collective-permute-start | bytes 700424 | tf_op jit(solution)/shard_map/ppermute | solution.py:89
  168.6 9.1 %collective-permute-start.39 = (f32[152,384]{1,0:T(8,128)S(1)}, f32[152,384]{1,0:T(8,128)S(1)}, u32[]{:S(2)}, u32[]{:S(2)}) collective-permute-start(f32[152,384]{1,0:T(8,128)S(1)} %fusion.8.mine), channel_id=1, source_target_pairs={{0,16},{2,18},{4,20},{6,22},{8,24},{10,26},{12,28},{14,30},{16,0},... | collective-permute-start | bytes 700424 | tf_op jit(solution)/shard_map/ppermute | solution.py:89
  178.1 9.4 %collective-permute-start.43 = (f32[152,384]{1,0:T(8,128)S(1)}, f32[152,384]{1,0:T(8,128)S(1)}, u32[]{:S(2)}, u32[]{:S(2)}) collective-permute-start(f32[152,384]{1,0:T(8,128)S(1)} %residual.3.refs_0_.refs_2_), channel_id=1, source_target_pairs={{0,4},{2,6},{4,0},{6,2},{8,12},{10,14},{12,8},{14,10},{16,20},{18,... | collective-permute-start | bytes 700424 | tf_op jit(solution)/shard_map/ppermute | solution.py:89
  181.7 12.2 %collective-permute-start.45 = (f32[152,384]{1,0:T(8,128)S(1)}, f32[152,384]{1,0:T(8,128)S(1)}, u32[]{:S(2)}, u32[]{:S(2)}) collective-permute-start(f32[152,384]{1,0:T(8,128)S(1)} %residual.3.refs_0_.refs_2_), channel_id=1, source_target_pairs={{0,2},{2,0},{4,6},{6,4},{8,10},{10,8},{12,14},{14,12},{16,18},{18,... | collective-permute-start | bytes 700424 | tf_op jit(solution)/shard_map/ppermute | solution.py:89
  184.1 9.8 %collective-permute-start.46 = (f32[152,384]{1,0:T(8,128)S(1)}, f32[152,384]{1,0:T(8,128)S(1)}, u32[]{:S(2)}, u32[]{:S(2)}) collective-permute-start(f32[152,384]{1,0:T(8,128)S(1)} %collective-permute-done.40.refs_0_), channel_id=1, source_target_pairs={{0,4},{2,6},{4,0},{6,2},{8,12},{10,14},{12,8},{14,10},{16,20},{18,... | collective-permute-start | bytes 700424 | tf_op jit(solution)/shard_map/ppermute | solution.py:89
  187.5 8.4 %collective-permute-start.44 = (f32[152,384]{1,0:T(8,128)S(1)}, f32[152,384]{1,0:T(8,128)S(1)}, u32[]{:S(2)}, u32[]{:S(2)}) collective-permute-start(f32[152,384]{1,0:T(8,128)S(1)} %collective-permute-done.43.refs_1_), channel_id=1, source_target_pairs={{0,2},{2,0},{4,6},{6,4},{8,10},{10,8},{12,14},{14,12},{16,18},{18,... | collective-permute-start | bytes 700424 | tf_op jit(solution)/shard_map/ppermute | solution.py:89
  (23 other events, 152.7 us)

commit v3 on v2

--- a/solution.py
+++ b/solution.py
@@ -375,7 +375,8 @@
 
 def next_scores(parts, look, groups, columns):
     after, own, found = look[1], [], {}
-    for group, (high, low) in zip(reversed(groups), reversed(parts)):
+    order = list(zip(groups, parts))
+    for group, (high, low) in order[:1:-1] + order[:2]:
         sums = scores_call(look, high, low, after, widths_of(group, columns))
         after = sums[0]
         for (unit, half), value in zip(group, sums):

time: 216 us -> 216 us (level)
  no operation moved by 1% of the time
where the time goes in v3:
time: 216 us; the launch traced here: 215 us
  Pallas kernels  75.2 us (35%)
  starting transfers between devices  57 us (26%)
  waiting for transfers between devices  53.1 us (25%)
  blocking collectives  22.3 us (10%)
  local copies, waits for them, and re-layouts  3.46 us (2%)
  other arithmetic  3.3 us (2%)
    ppermute x42, starting transfers between devices, swap(): return lax.ppermute(value, axis, [(i, i ^ 1 << bit) for i in range(count)])  50 us
    ppermute x42, waiting for transfers between devices, swap(): return lax.ppermute(value, axis, [(i, i ^ 1 << bit) for i in range(count)])  46.5 us
    pallas_call x5, Pallas kernels, features_call(): pl.pallas_call(functools.partial(features_kernel, arrays=len(frames), aft...  44.1 us
    all_to_all x2, blocking collectives, on_device(): tiles = lax.all_to_all(tiles, 'feat', 0, 0)  22.3 us
    pallas_call x12, Pallas kernels, gradient_call(): pl.pallas_call(functools.partial(gradient_kernel, halves=halves, first=fi...  17.9 us
    pallas_call x5, Pallas kernels, scores_call(): pl.pallas_call(scores_kernel, in_specs=[whole] * 4 + [pl.BlockSpec(memory...  8.74 us
    ppermute x7, starting transfers between devices, first_scores(): lax.ppermute(value, 'feat', [(i, i ^ unit) for i in range(count)])  6.97 us
    ppermute x7, waiting for transfers between devices, first_scores(): lax.ppermute(value, 'feat', [(i, i ^ unit) for i in range(count)])  6.67 us
  transfers between devices with their start and end apart: 49, of which 19 were waited for; matrix products, arithmetic and copies ran while one was open for 2% of the time, Pallas kernels for 32%

profile of v3, /device:TPU:0, one launch (start us, length us, event | category | flops | bytes accessed | tf_op | source)
XLA Modules:
  0.0 215.4 jit_solution(10103714613510085940)
XLA Ops:
  0.6 4.1 %collective-permute-start.1 = (f32[192,440]{1,0:T(8,128)}, f32[192,440]{1,0:T(8,128)S(1)}, u32[]{:S(2)}, u32[]{:S(2)}) collective-permute-start(f32[192,440]{1,0:T(8,128)} %refs_0_.1), channel_id=1, source_target_pairs={{0,16},{2,18},{4,20},{6,22},{8,24},{10,26},{12,28},{14,30},{16,0},... | collective-permute-start | bytes 1013768 | tf_op jit(solution)/shard_map/ppermute | solution.py:89
  13.2 2.8 %fusion = (bf16[440,2048]{1,0:T(8,128)(2,1)S(1)}, bf16[440,2048]{1,0:T(8,128)(2,1)S(1)}) fusion(f32[440,2048]{1,0:T(8,128)} %param.8), kind=kLoop, calls=%fused_computation.2 | loop fusion | flops 4505600 | bytes 7208960 | tf_op jit(solution)/shard_map/convert_element_type | solution.py:45
  16.1 6.5 %collective-permute-done.1.refs_4_ = f32[192,440]{1,0:T(8,128)S(1)} collective-permute-done((f32[192,440]{1,0:T(8,128)}, f32[192,440]{1,0:T(8,128)S(1)}, u32[]{:S(2)}, u32[]{:S(2)}) %collective-permute-start.1) | collective-permute-done | bytes 337952 | tf_op jit(solution)/shard_map/ppermute | solution.py:89
  24.8 3.7 %features.5 = (bf16[192,2048]{1,0:T(8,128)(2,1)S(1)}, bf16[192,2048]{1,0:T(8,128)(2,1)S(1)}, f32[152,192]{1,0:T(8,128)S(1)}) custom-call(f32[192,440]{1,0:T(8,128)S(1)} %copy-done.4, bf16[440,2048]{1,0:T(8,128)(2,1)S(1)} %get-tuple-element.79.refs_1_.refs_5_.refs_4_.refs_2_, bf16[440,2048]{1,0:T(8,128)(2,1)S(1)} %get-tuple-element.78.refs_2_.refs_6_.refs_5_.refs_3_, ...), custom_call_target="tpu_custom_call" | custom-call | flops 1862270976 | bytes 1572864 | tf_op jit(solution)/shard_map/features/pallas_call | solution.py:167
  30.7 2.2 %collective-permute-done.4.refs_3_ = f32[192,440]{1,0:T(8,128)S(1)} collective-permute-done((f32[192,440]{1,0:T(8,128)S(1)}, f32[192,440]{1,0:T(8,128)S(1)}, u32[]{:S(2)}, u32[]{:S(2)}) %collective-permute-start.4) | collective-permute-done | bytes 337952 | tf_op jit(solution)/shard_map/ppermute | solution.py:89
  34.1 1.8 collective-permute-start.10
  35.9 13.1 %features.6 = (bf16[960,2048]{1,0:T(8,128)(2,1)S(1)}, bf16[960,2048]{1,0:T(8,128)(2,1)S(1)}, f32[152,384]{1,0:T(8,128)S(1)}, f32[152,384]{1,0:T(8,128)S(1)}, f32[152,192]{1,0:T(8,128)S(1)}) custom-call(f32[192,440]{1,0:T(8,128)S(1)} %collective-permute-done.refs_0_, f32[192,440]{1,0:T(8,128)S(1)} %collective-permute-done.2.refs_1_, ...), custom_call_target="tpu_custom_call" | custom-call | flops 9311354880 | bytes 7864320 | tf_op jit(solution)/shard_map/features/pallas_call | solution.py:167
  54.6 10.6 %features.7 = (bf16[768,2048]{1,0:T(8,128)(2,1)S(1)}, bf16[768,2048]{1,0:T(8,128)(2,1)S(1)}, f32[152,384]{1,0:T(8,128)S(1)}, f32[152,384]{1,0:T(8,128)S(1)}) custom-call(f32[192,440]{1,0:T(8,128)S(1)} %collective-permute-done.7.refs_0_, f32[192,440]{1,0:T(8,128)S(1)} %collective-permute-done.8.refs_1_, f32[192,440]{1,0:T(8,128)S(1)} %collective-permute-done.9.refs_2_, ...), custom_call_target="tpu_custom_call" | custom-call | flops 7449083904 | bytes 6291456 | tf_op jit(solution)/shard_map/features/pallas_call | solution.py:167
  69.0 10.6 %features.8 = (bf16[768,2048]{1,0:T(8,128)(2,1)S(1)}, bf16[768,2048]{1,0:T(8,128)(2,1)S(1)}, f32[152,384]{1,0:T(8,128)S(1)}, f32[152,384]{1,0:T(8,128)S(1)}) custom-call(f32[192,440]{1,0:T(8,128)S(1)} %collective-permute-done.13.refs_0_, f32[192,440]{1,0:T(8,128)S(1)} %collective-permute-done.14.refs_1_, f32[192,440]{1,0:T(8,128)S(1)} %collective-permute-done.15.refs_2_, ...), custom_call_target="tpu_custom_call" | custom-call | flops 7449083904 | bytes 6291456 | tf_op jit(solution)/shard_map/features/pallas_call | solution.py:167
  79.6 1.8 collective-permute-start.18
  82.9 6.2 %features.9 = (bf16[384,2048]{1,0:T(8,128)(2,1)S(1)}, bf16[384,2048]{1,0:T(8,128)(2,1)S(1)}, f32[152,384]{1,0:T(8,128)S(1)}) custom-call(f32[192,440]{1,0:T(8,128)S(1)} %collective-permute-done.19.refs_0_, f32[192,440]{1,0:T(8,128)S(1)} %collective-permute-done.20.refs_1_, bf16[440,2048]{1,0:T(8,128)(2,1)S(1)} %get-tuple-element.79.refs_1_.refs_5_.refs_4_.refs_2_, ...), custom_call_target="tpu_custom_call" | custom-call | flops 3724541952 | bytes 3145728 | tf_op jit(solution)/shard_map/features/pallas_call | solution.py:167
  91.9 5.1 %collective-permute-done.21 = f32[152,384]{1,0:T(8,128)S(1)} collective-permute-done((f32[152,384]{1,0:T(8,128)S(1)}, f32[152,384]{1,0:T(8,128)S(1)}, u32[]{:S(2)}, u32[]{:S(2)}) %collective-permute-start.21) | collective-permute-done | bytes 233504 | tf_op jit(solution)/shard_map/ppermute | solution.py:371
  97.2 5.2 %collective-permute-start.22 = (f32[152,384]{1,0:T(8,128)S(1)}, f32[152,384]{1,0:T(8,128)S(1)}, u32[]{:S(2)}, u32[]{:S(2)}) collective-permute-start(f32[152,384]{1,0:T(8,128)S(1)} %fusion.6.mine), channel_id=1, source_target_pairs={{0,16},{2,18},{4,20},{6,22},{8,24},{10,26},{12,28},{14,30},{16,0},... | collective-permute-start | bytes 700424 | tf_op jit(solution)/shard_map/ppermute | solution.py:89
  102.4 5.4 %collective-permute-done.22.theirs = f32[152,384]{1,0:T(8,128)S(1)} collective-permute-done((f32[152,384]{1,0:T(8,128)S(1)}, f32[152,384]{1,0:T(8,128)S(1)}, u32[]{:S(2)}, u32[]{:S(2)}) %collective-permute-start.22) | collective-permute-done | bytes 233504 | tf_op jit(solution)/shard_map/ppermute | solution.py:89
  110.3 3.9 %collective-permute-done.23.refs_0_ = f32[152,384]{1,0:T(8,128)S(1)} collective-permute-done((f32[152,384]{1,0:T(8,128)S(1)}, f32[152,384]{1,0:T(8,128)S(1)}, u32[]{:S(2)}, u32[]{:S(2)}) %collective-permute-start.23) | collective-permute-done | bytes 233504 | tf_op jit(solution)/shard_map/ppermute | solution.py:89
  117.9 2.7 %gradient.13.refs_4_ = f32[152,2048]{1,0:T(8,128)S(1)} custom-call(f32[152,384]{1,0:T(8,128)S(1)} %collective-permute-done.23.refs_0_, f32[152,384]{1,0:T(8,128)S(1)} %collective-permute-done.26.refs_1_, f32[152,384]{1,0:T(8,128)S(1)} %residual.2.refs_0_.refs_2_, ...), custom_call_target="tpu_custom_call", output_to_operand_aliasing={{}: (5, {})} | custom-call | flops 2390753280 | bytes 7864320 | tf_op jit(solution)/shard_map/gradient/pallas_call | solution.py:238
  122.6 2.0 gradient.14.refs_4_
  124.6 2.0 gradient.15.refs_3_
  132.3 11.2 %all_to_all.10.tiles = f32[16,8,128]{2,1,0:T(8,128)S(1)} all-to-all(f32[16,8,128]{2,1,0:T(8,128)S(1)} %get-tuple-element.61), channel_id=1, replica_groups=mesh['feat'=16,'frame'=2] {'feat'}, dimensions={0} | all-to-all | bytes 131072 | tf_op jit(solution)/shard_map/all_to_all | solution.py:425
  146.5 2.0 scores.6
  149.1 2.0 scores.7
  155.8 2.7 %scores.9 = (f32[152,384]{1,0:T(8,128)S(1)}, f32[152,384]{1,0:T(8,128)S(1)}, f32[152,192]{1,0:T(8,128)S(1)}) custom-call(bf16[304,2048]{1,0:T(8,128)(2,1)S(1)} %get-tuple-element.63.look, bf16[152,2048]{1,0:T(8,128)(2,1)S(1)} %get-tuple-element.64.look_high._, bf16[960,2048]{1,0:T(8,128)(2,1)S(1)} %get-tuple-element.57.refs_3_.high, ...), custom_call_target="tpu_custom_call" | custom-call | flops 2390753280 | bytes 7864320 | tf_op jit(solution)/shard_map/scores/pallas_call | solution.py:192
  159.0 2.6 %collective-permute-done.33 = f32[152,384]{1,0:T(8,128)S(1)} collective-permute-done((f32[152,384]{1,0:T(8,128)S(1)}, f32[152,384]{1,0:T(8,128)S(1)}, u32[]{:S(2)}, u32[]{:S(2)}) %collective-permute-start.33) | collective-permute-done | bytes 233504 | tf_op jit(solution)/shard_map/ppermute | solution.py:89
  162.1 2.8 %collective-permute-done.36 = f32[152,384]{1,0:T(8,128)S(1)} collective-permute-done((f32[152,384]{1,0:T(8,128)S(1)}, f32[152,384]{1,0:T(8,128)S(1)}, u32[]{:S(2)}, u32[]{:S(2)}) %collective-permute-start.36) | collective-permute-done | bytes 233504 | tf_op jit(solution)/shard_map/ppermute | solution.py:89
  164.9 3.7 %collective-permute-done.35 = f32[152,384]{1,0:T(8,128)S(1)} collective-permute-done((f32[152,384]{1,0:T(8,128)S(1)}, f32[152,384]{1,0:T(8,128)S(1)}, u32[]{:S(2)}, u32[]{:S(2)}) %collective-permute-start.35) | collective-permute-done | bytes 233504 | tf_op jit(solution)/shard_map/ppermute | solution.py:89
  168.8 9.0 %collective-permute-done.39.theirs = f32[152,384]{1,0:T(8,128)S(1)} collective-permute-done((f32[152,384]{1,0:T(8,128)S(1)}, f32[152,384]{1,0:T(8,128)S(1)}, u32[]{:S(2)}, u32[]{:S(2)}) %collective-permute-start.39) | collective-permute-done | bytes 233504 | tf_op jit(solution)/shard_map/ppermute | solution.py:89
  178.1 3.6 %collective-permute-start.43 = (f32[152,384]{1,0:T(8,128)S(1)}, f32[152,384]{1,0:T(8,128)S(1)}, u32[]{:S(2)}, u32[]{:S(2)}) collective-permute-start(f32[152,384]{1,0:T(8,128)S(1)} %residual.3.refs_0_.refs_2_), channel_id=1, source_target_pairs={{0,4},{2,6},{4,0},{6,2},{8,12},{10,14},{12,8},{14,10},{16,20},{18,... | collective-permute-start | bytes 700424 | tf_op jit(solution)/shard_map/ppermute | solution.py:89
  181.7 2.4 %collective-permute-done.40.refs_0_ = f32[152,384]{1,0:T(8,128)S(1)} collective-permute-done((f32[152,384]{1,0:T(8,128)S(1)}, f32[152,384]{1,0:T(8,128)S(1)}, u32[]{:S(2)}, u32[]{:S(2)}) %collective-permute-start.40) | collective-permute-done | bytes 233504 | tf_op jit(solution)/shard_map/ppermute | solution.py:89
  188.7 2.6 %gradient.19.refs_4_ = f32[152,2048]{1,0:T(8,128)S(1)} custom-call(f32[152,384]{1,0:T(8,128)S(1)} %collective-permute-done.40.refs_0_, f32[152,384]{1,0:T(8,128)S(1)} %collective-permute-done.43.refs_1_, f32[152,384]{1,0:T(8,128)S(1)} %residual.3.refs_0_.refs_2_, ...), custom_call_target="tpu_custom_call", output_to_operand_aliasing={{}: (5, {})} | custom-call | flops 2390753280 | bytes 7864320 | tf_op jit(solution)/shard_map/gradient/pallas_call | solution.py:238
  193.9 2.0 gradient.20.refs_4_
  196.0 2.2 %gradient.21.refs_3_ = f32[152,2048]{1,0:T(8,128)S(1)} custom-call(f32[152,384]{1,0:T(8,128)S(1)} %collective-permute-done.44.refs_0_, f32[152,384]{1,0:T(8,128)S(1)} %collective-permute-done.41.refs_1_, bf16[768,2048]{1,0:T(8,128)(2,1)S(1)} %get-tuple-element.53.refs_2_.high, ...), custom_call_target="tpu_custom_call", output_to_operand_aliasing={{}: (4, {})} | custom-call | flops 1912602624 | bytes 6291456 | tf_op jit(solution)/shard_map/gradient/pallas_call | solution.py:238
  202.5 11.1 %all_to_all.11.tiles = f32[16,8,128]{2,1,0:T(8,128)S(1)} all-to-all(f32[16,8,128]{2,1,0:T(8,128)S(1)} %get-tuple-element.72), channel_id=1, replica_groups=mesh['feat'=16,'frame'=2] {'feat'}, dimensions={0} | all-to-all | bytes 131072 | tf_op jit(solution)/shard_map/all_to_all | solution.py:425
  (119 shorter events, 64.7 us)
Async XLA Ops:
  0.6 22.0 %collective-permute-start.1 = (f32[192,440]{1,0:T(8,128)}, f32[192,440]{1,0:T(8,128)S(1)}, u32[]{:S(2)}, u32[]{:S(2)}) collective-permute-start(f32[192,440]{1,0:T(8,128)} %refs_0_.1), channel_id=1, source_target_pairs={{0,16},{2,18},{4,20},{6,22},{8,24},{10,26},{12,28},{14,30},{16,0},... | collective-permute-start | bytes 1013768 | tf_op jit(solution)/shard_map/ppermute | solution.py:89
  4.7 23.8 %collective-permute-start = (f32[192,440]{1,0:T(8,128)}, f32[192,440]{1,0:T(8,128)S(1)}, u32[]{:S(2)}, u32[]{:S(2)}) collective-permute-start(f32[192,440]{1,0:T(8,128)} %refs_0_.1), channel_id=1, source_target_pairs={{0,8},{2,10},{4,12},{6,14},{8,0},{10,2},{12,4},{14,6},{16,24},{18,... | collective-permute-start | bytes 1013768 | tf_op jit(solution)/shard_map/ppermute | solution.py:89
  6.3 42.6 %collective-permute-start.7 = (f32[192,440]{1,0:T(8,128)}, f32[192,440]{1,0:T(8,128)S(1)}, u32[]{:S(2)}, u32[]{:S(2)}) collective-permute-start(f32[192,440]{1,0:T(8,128)} %refs_0_.1), channel_id=1, source_target_pairs={{0,2},{2,0},{4,6},{6,4},{8,10},{10,8},{12,14},{14,12},{16,18},{18,... | collective-permute-start | bytes 1013768 | tf_op jit(solution)/shard_map/ppermute | solution.py:89
  7.8 22.3 %collective-permute-start.3 = (f32[192,440]{1,0:T(8,128)}, f32[192,440]{1,0:T(8,128)S(1)}, u32[]{:S(2)}, u32[]{:S(2)}) collective-permute-start(f32[192,440]{1,0:T(8,128)} %refs_0_.1), channel_id=1, source_target_pairs={{0,4},{2,6},{4,0},{6,2},{8,12},{10,14},{12,8},{14,10},{16,20},{18,... | collective-permute-start | bytes 1013768 | tf_op jit(solution)/shard_map/ppermute | solution.py:89
  22.6 10.2 %collective-permute-start.4 = (f32[192,440]{1,0:T(8,128)S(1)}, f32[192,440]{1,0:T(8,128)S(1)}, u32[]{:S(2)}, u32[]{:S(2)}) collective-permute-start(f32[192,440]{1,0:T(8,128)S(1)} %collective-permute-done.1.refs_4_), channel_id=1, source_target_pairs={{0,4},{2,6},{4,0},{6,2},{8,12},{10,14},{12,8},{14,10},{16,20},{18,... | collective-permute-start | bytes 1013768 | tf_op jit(solution)/shard_map/ppermute | solution.py:89
  24.2 9.9 %collective-permute-start.2 = (f32[192,440]{1,0:T(8,128)S(1)}, f32[192,440]{1,0:T(8,128)S(1)}, u32[]{:S(2)}, u32[]{:S(2)}) collective-permute-start(f32[192,440]{1,0:T(8,128)S(1)} %collective-permute-done.1.refs_4_), channel_id=1, source_target_pairs={{0,8},{2,10},{4,12},{6,14},{8,0},{10,2},{12,4},{14,6},{16,24},{18,... | collective-permute-start | bytes 1013768 | tf_op jit(solution)/shard_map/ppermute | solution.py:89
  28.6 22.0 %collective-permute-start.8 = (f32[192,440]{1,0:T(8,128)S(1)}, f32[192,440]{1,0:T(8,128)S(1)}, u32[]{:S(2)}, u32[]{:S(2)}) collective-permute-start(f32[192,440]{1,0:T(8,128)S(1)} %collective-permute-done.1.refs_4_), channel_id=1, source_target_pairs={{0,2},{2,0},{4,6},{6,4},{8,10},{10,8},{12,14},{14,12},{16,18},{18,... | collective-permute-start | bytes 1013768 | tf_op jit(solution)/shard_map/ppermute | solution.py:89
  30.1 20.9 %collective-permute-start.15 = (f32[192,440]{1,0:T(8,128)S(1)}, f32[192,440]{1,0:T(8,128)S(1)}, u32[]{:S(2)}, u32[]{:S(2)}) collective-permute-start(f32[192,440]{1,0:T(8,128)S(1)} %collective-permute-done.refs_0_), channel_id=1, source_target_pairs={{0,2},{2,0},{4,6},{6,4},{8,10},{10,8},{12,14},{14,12},{16,18},{18,... | collective-permute-start | bytes 1013768 | tf_op jit(solution)/shard_map/ppermute | solution.py:89
  32.8 18.5 %collective-permute-start.9 = (f32[192,440]{1,0:T(8,128)S(1)}, f32[192,440]{1,0:T(8,128)S(1)}, u32[]{:S(2)}, u32[]{:S(2)}) collective-permute-start(f32[192,440]{1,0:T(8,128)S(1)} %collective-permute-done.refs_0_), channel_id=1, source_target_pairs={{0,4},{2,6},{4,0},{6,2},{8,12},{10,14},{12,8},{14,10},{16,20},{18,... | collective-permute-start | bytes 1013768 | tf_op jit(solution)/shard_map/ppermute | solution.py:89
  34.1 18.9 %collective-permute-start.10 = (f32[192,440]{1,0:T(8,128)S(1)}, f32[192,440]{1,0:T(8,128)S(1)}, u32[]{:S(2)}, u32[]{:S(2)}) collective-permute-start(f32[192,440]{1,0:T(8,128)S(1)} %collective-permute-done.4.refs_3_), channel_id=1, source_target_pairs={{0,8},{2,10},{4,12},{6,14},{8,0},{10,2},{12,4},{14,6},{16,24},{18,... | collective-permute-start | bytes 1013768 | tf_op jit(solution)/shard_map/ppermute | solution.py:89
  49.0 16.2 %collective-permute-start.13 = (f32[192,440]{1,0:T(8,128)S(1)}, f32[192,440]{1,0:T(8,128)S(1)}, u32[]{:S(2)}, u32[]{:S(2)}) collective-permute-start(f32[192,440]{1,0:T(8,128)S(1)} %collective-permute-done.3.refs_2_), channel_id=1, source_target_pairs={{0,2},{2,0},{4,6},{6,4},{8,10},{10,8},{12,14},{14,12},{16,18},{18,... | collective-permute-start | bytes 1013768 | tf_op jit(solution)/shard_map/ppermute | solution.py:89
  50.5 15.3 %collective-permute-start.6 = (f32[152,384]{1,0:T(8,128)S(1)}, f32[152,384]{1,0:T(8,128)S(1)}, u32[]{:S(2)}, u32[]{:S(2)}) collective-permute-start(f32[152,384]{1,0:T(8,128)S(1)} %get-tuple-element.45), channel_id=1, source_target_pairs={{0,4},{2,6},{4,0},{6,2},{8,12},{10,14},{12,8},{14,10},{16,20},{18,... | collective-permute-start | bytes 700424 | tf_op jit(solution)/shard_map/ppermute | solution.py:371
  51.0 15.2 %collective-permute-start.5 = (f32[152,384]{1,0:T(8,128)S(1)}, f32[152,384]{1,0:T(8,128)S(1)}, u32[]{:S(2)}, u32[]{:S(2)}) collective-permute-start(f32[152,384]{1,0:T(8,128)S(1)} %get-tuple-element.44.refs_9_), channel_id=1, source_target_pairs={{0,8},{2,10},{4,12},{6,14},{8,0},{10,2},{12,4},{14,6},{16,24},{18,... | collective-permute-start | bytes 700424 | tf_op jit(solution)/shard_map/ppermute | solution.py:371
  51.3 16.2 %collective-permute-start.16 = (f32[192,440]{1,0:T(8,128)S(1)}, f32[192,440]{1,0:T(8,128)S(1)}, u32[]{:S(2)}, u32[]{:S(2)}) collective-permute-start(f32[192,440]{1,0:T(8,128)S(1)} %collective-permute-done.8.refs_1_), channel_id=1, source_target_pairs={{0,8},{2,10},{4,12},{6,14},{8,0},{10,2},{12,4},{14,6},{16,24},{18,... | collective-permute-start | bytes 1013768 | tf_op jit(solution)/shard_map/ppermute | solution.py:89
  53.1 16.0 %collective-permute-start.14 = (f32[192,440]{1,0:T(8,128)S(1)}, f32[192,440]{1,0:T(8,128)S(1)}, u32[]{:S(2)}, u32[]{:S(2)}) collective-permute-start(f32[192,440]{1,0:T(8,128)S(1)} %collective-permute-done.8.refs_1_), channel_id=1, source_target_pairs={{0,4},{2,6},{4,0},{6,2},{8,12},{10,14},{12,8},{14,10},{16,20},{18,... | collective-permute-start | bytes 1013768 | tf_op jit(solution)/shard_map/ppermute | solution.py:89
  65.2 16.2 %collective-permute-start.19 = (f32[192,440]{1,0:T(8,128)S(1)}, f32[192,440]{1,0:T(8,128)S(1)}, u32[]{:S(2)}, u32[]{:S(2)}) collective-permute-start(f32[192,440]{1,0:T(8,128)S(1)} %collective-permute-done.9.refs_2_), channel_id=1, source_target_pairs={{0,2},{2,0},{4,6},{6,4},{8,10},{10,8},{12,14},{14,12},{16,18},{18,... | collective-permute-start | bytes 1013768 | tf_op jit(solution)/shard_map/ppermute | solution.py:89
  65.8 17.1 %collective-permute-start.12 = (f32[152,384]{1,0:T(8,128)S(1)}, f32[152,384]{1,0:T(8,128)S(1)}, u32[]{:S(2)}, u32[]{:S(2)}) collective-permute-start(f32[152,384]{1,0:T(8,128)S(1)} %get-tuple-element.47), channel_id=1, source_target_pairs={{0,12},{2,14},{4,8},{6,10},{8,4},{10,6},{12,0},{14,2},{16,28},{18,... | collective-permute-start | bytes 700424 | tf_op jit(solution)/shard_map/ppermute | solution.py:371
  66.3 16.6 %collective-permute-start.11 = (f32[152,384]{1,0:T(8,128)S(1)}, f32[152,384]{1,0:T(8,128)S(1)}, u32[]{:S(2)}, u32[]{:S(2)}) collective-permute-start(f32[152,384]{1,0:T(8,128)S(1)} %get-tuple-element.46.refs_9_), channel_id=1, source_target_pairs={{0,2},{2,0},{4,6},{6,4},{8,10},{10,8},{12,14},{14,12},{16,18},{18,... | collective-permute-start | bytes 700424 | tf_op jit(solution)/shard_map/ppermute | solution.py:371
  67.5 15.4 %collective-permute-start.20 = (f32[192,440]{1,0:T(8,128)S(1)}, f32[192,440]{1,0:T(8,128)S(1)}, u32[]{:S(2)}, u32[]{:S(2)}) collective-permute-start(f32[192,440]{1,0:T(8,128)S(1)} %collective-permute-done.16.refs_3_), channel_id=1, source_target_pairs={{0,4},{2,6},{4,0},{6,2},{8,12},{10,14},{12,8},{14,10},{16,20},{18,... | collective-permute-start | bytes 1013768 | tf_op jit(solution)/shard_map/ppermute | solution.py:89
  79.6 10.7 %collective-permute-start.18 = (f32[152,384]{1,0:T(8,128)S(1)}, f32[152,384]{1,0:T(8,128)S(1)}, u32[]{:S(2)}, u32[]{:S(2)}) collective-permute-start(f32[152,384]{1,0:T(8,128)S(1)} %get-tuple-element.49), channel_id=1, source_target_pairs={{0,10},{2,8},{4,14},{6,12},{8,2},{10,0},{12,6},{14,4},{16,26},{18,... | collective-permute-start | bytes 700424 | tf_op jit(solution)/shard_map/ppermute | solution.py:371
  81.4 10.4 %collective-permute-start.17 = (f32[152,384]{1,0:T(8,128)S(1)}, f32[152,384]{1,0:T(8,128)S(1)}, u32[]{:S(2)}, u32[]{:S(2)}) collective-permute-start(f32[152,384]{1,0:T(8,128)S(1)} %get-tuple-element.48.refs_7_), channel_id=1, source_target_pairs={{0,6},{2,4},{4,2},{6,0},{8,14},{10,12},{12,10},{14,8},{16,22},{18,... | collective-permute-start | bytes 700424 | tf_op jit(solution)/shard_map/ppermute | solution.py:371
  97.2 10.7 %collective-permute-start.22 = (f32[152,384]{1,0:T(8,128)S(1)}, f32[152,384]{1,0:T(8,128)S(1)}, u32[]{:S(2)}, u32[]{:S(2)}) collective-permute-start(f32[152,384]{1,0:T(8,128)S(1)} %fusion.6.mine), channel_id=1, source_target_pairs={{0,16},{2,18},{4,20},{6,22},{8,24},{10,26},{12,28},{14,30},{16,0},... | collective-permute-start | bytes 700424 | tf_op jit(solution)/shard_map/ppermute | solution.py:89
  108.2 9.0 %collective-permute-start.26 = (f32[152,384]{1,0:T(8,128)S(1)}, f32[152,384]{1,0:T(8,128)S(1)}, u32[]{:S(2)}, u32[]{:S(2)}) collective-permute-start(f32[152,384]{1,0:T(8,128)S(1)} %residual.2.refs_0_.refs_2_), channel_id=1, source_target_pairs={{0,4},{2,6},{4,0},{6,2},{8,12},{10,14},{12,8},{14,10},{16,20},{18,... | collective-permute-start | bytes 700424 | tf_op jit(solution)/shard_map/ppermute | solution.py:89
  108.9 13.7 %collective-permute-start.28 = (f32[152,384]{1,0:T(8,128)S(1)}, f32[152,384]{1,0:T(8,128)S(1)}, u32[]{:S(2)}, u32[]{:S(2)}) collective-permute-start(f32[152,384]{1,0:T(8,128)S(1)} %residual.2.refs_0_.refs_2_), channel_id=1, source_target_pairs={{0,2},{2,0},{4,6},{6,4},{8,10},{10,8},{12,14},{14,12},{16,18},{18,... | collective-permute-start | bytes 700424 | tf_op jit(solution)/shard_map/ppermute | solution.py:89
  148.5 10.0 %collective-permute-start.37 = (f32[152,384]{1,0:T(8,128)S(1)}, f32[152,384]{1,0:T(8,128)S(1)}, u32[]{:S(2)}, u32[]{:S(2)}) collective-permute-start(f32[152,384]{1,0:T(8,128)S(1)} %get-tuple-element.65._), channel_id=1, source_target_pairs={{0,2},{2,0},{4,6},{6,4},{8,10},{10,8},{12,14},{14,12},{16,18},{18,... | collective-permute-start | bytes 700424 | tf_op jit(solution)/shard_map/ppermute | solution.py:89
  152.9 8.7 %collective-permute-start.33 = (f32[152,384]{1,0:T(8,128)S(1)}, f32[152,384]{1,0:T(8,128)S(1)}, u32[]{:S(2)}, u32[]{:S(2)}) collective-permute-start(f32[152,384]{1,0:T(8,128)S(1)} %add.57), channel_id=1, source_target_pairs={{0,2},{2,0},{4,6},{6,4},{8,10},{10,8},{12,14},{14,12},{16,18},{18,... | collective-permute-start | bytes 700424 | tf_op jit(solution)/shard_map/ppermute | solution.py:89
  154.9 9.9 %collective-permute-start.36 = (f32[152,384]{1,0:T(8,128)S(1)}, f32[152,384]{1,0:T(8,128)S(1)}, u32[]{:S(2)}, u32[]{:S(2)}) collective-permute-start(f32[152,384]{1,0:T(8,128)S(1)} %get-tuple-element.66._), channel_id=1, source_target_pairs={{0,2},{2,0},{4,6},{6,4},{8,10},{10,8},{12,14},{14,12},{16,18},{18,... | collective-permute-start | bytes 700424 | tf_op jit(solution)/shard_map/ppermute | solution.py:89
  168.7 9.1 %collective-permute-start.39 = (f32[152,384]{1,0:T(8,128)S(1)}, f32[152,384]{1,0:T(8,128)S(1)}, u32[]{:S(2)}, u32[]{:S(2)}) collective-permute-start(f32[152,384]{1,0:T(8,128)S(1)} %fusion.8.mine), channel_id=1, source_target_pairs={{0,16},{2,18},{4,20},{6,22},{8,24},{10,26},{12,28},{14,30},{16,0},... | collective-permute-start | bytes 700424 | tf_op jit(solution)/shard_map/ppermute | solution.py:89
  178.1 9.4 %collective-permute-start.43 = (f32[152,384]{1,0:T(8,128)S(1)}, f32[152,384]{1,0:T(8,128)S(1)}, u32[]{:S(2)}, u32[]{:S(2)}) collective-permute-start(f32[152,384]{1,0:T(8,128)S(1)} %residual.3.refs_0_.refs_2_), channel_id=1, source_target_pairs={{0,4},{2,6},{4,0},{6,2},{8,12},{10,14},{12,8},{14,10},{16,20},{18,... | collective-permute-start | bytes 700424 | tf_op jit(solution)/shard_map/ppermute | solution.py:89
  181.7 12.3 %collective-permute-start.45 = (f32[152,384]{1,0:T(8,128)S(1)}, f32[152,384]{1,0:T(8,128)S(1)}, u32[]{:S(2)}, u32[]{:S(2)}) collective-permute-start(f32[152,384]{1,0:T(8,128)S(1)} %residual.3.refs_0_.refs_2_), channel_id=1, source_target_pairs={{0,2},{2,0},{4,6},{6,4},{8,10},{10,8},{12,14},{14,12},{16,18},{18,... | collective-permute-start | bytes 700424 | tf_op jit(solution)/shard_map/ppermute | solution.py:89
  184.1 9.8 %collective-permute-start.46 = (f32[152,384]{1,0:T(8,128)S(1)}, f32[152,384]{1,0:T(8,128)S(1)}, u32[]{:S(2)}, u32[]{:S(2)}) collective-permute-start(f32[152,384]{1,0:T(8,128)S(1)} %collective-permute-done.40.refs_0_), channel_id=1, source_target_pairs={{0,4},{2,6},{4,0},{6,2},{8,12},{10,14},{12,8},{14,10},{16,20},{18,... | collective-permute-start | bytes 700424 | tf_op jit(solution)/shard_map/ppermute | solution.py:89
  187.5 8.4 %collective-permute-start.44 = (f32[152,384]{1,0:T(8,128)S(1)}, f32[152,384]{1,0:T(8,128)S(1)}, u32[]{:S(2)}, u32[]{:S(2)}) collective-permute-start(f32[152,384]{1,0:T(8,128)S(1)} %collective-permute-done.43.refs_1_), channel_id=1, source_target_pairs={{0,2},{2,0},{4,6},{6,4},{8,10},{10,8},{12,14},{14,12},{16,18},{18,... | collective-permute-start | bytes 700424 | tf_op jit(solution)/shard_map/ppermute | solution.py:89
  (23 other events, 152.4 us)
